TPU v7x, 32 devices: a whole 2x2x4 slice. The times are simulated.
32 devices in a mesh: replica: 8 (over z, core), tile: 4 (over y, x).
Axes of the slice: x: 2, y: 2, z: 4, core: 2. Of those that a mesh axis runs over, the one named last changes fastest.
Arguments:
- public_tokens: bfloat16 [2048, 5120], P('replica', 'tile'), may hold values from -6 to 6
- public_targets: bfloat16 [2048, 4096], P(('replica', 'tile')), may hold values from -6 to 6
- private_tokens: bfloat16 [3072, 5120], P('replica', 'tile'), may hold values from -6 to 6
- private_targets: bfloat16 [3072, 4096], P(('replica', 'tile')), may hold values from -6 to 6
- token_counts: int32 [8, 3], P('replica'), may hold values from 1 to 128, 320 in all within a row
- weight: float32 [5120, 4096], P('tile', 'replica'), may hold values from -0.078125 to 0.078125
- public_moment: float32 [5120, 4096], P('tile', 'replica'), may hold values from 1 to 10
- adam_first: float32 [5120, 4096], P('tile', 'replica'), may hold values from -3 to 3
- adam_second: float32 [5120, 4096], P('tile', 'replica'), may hold values from 0.1 to 1
- noise_draw: float32 [5120, 4096], P('tile', 'replica'), may hold values from -6 to 6
Outputs:
- new_weight: float32 [5120, 4096], P('tile', 'replica')
- new_first: float32 [5120, 4096], P('tile', 'replica')
- new_second: float32 [5120, 4096], P('tile', 'replica')
- new_public: float32 [5120, 4096], P('tile', 'replica')
Inputs may be any that keep to these rules, and one draw needn't show every extreme that they name: `token_counts`: each row holds the live token counts of one replica's 3 private examples; every row sums to 320 and its largest entry is 128.
All inputs are finite; a program needn't handle non-finite values.
Results may differ from a plain program's by a relative error of at most 0.0031.
Values may be sent and summed in bfloat16 or wider, within the bound.
A program may use at most 128 MiB of HBM per device.

v0:
```python
import math

import jax
import jax.numpy as jnp
from jax import lax
from jax.sharding import PartitionSpec as P

D = 5120
L = 128
Q = 4096


beta_first = 0.9
beta_second = 0.99
beta_public = 0.9
public_epsilon = 0.001
adam_epsilon = 1e-08
clip_factor = 0.6
noise_level = 4.0
learn_rate = 0.01
contract_rows = (((0,), (0,)), ((), ()))


def slot_owner(first_row, span, seq_len):
    rows_at = first_row + jnp.arange(span, dtype=jnp.int32)
    return (rows_at, rows_at // seq_len)


def per_slot(owners, values):
    picks = jnp.arange(values.shape[0], dtype=jnp.int32)
    return jnp.sum(jnp.where(owners[:, None] == picks[None, :], values[None, :], 0), axis=1)


def live_slots(first_row, span, counts_row, seq_len):
    rows_at, owners = slot_owner(first_row, span, seq_len)
    return rows_at % seq_len < per_slot(owners, counts_row)


def on_device(
    public_tokens,
    public_targets,
    private_tokens,
    private_targets,
    token_counts,
    weight,
    public_moment,
    adam_first,
    adam_second,
    noise_draw,
):
    replicas = lax.axis_size("replica")
    tile_pos = lax.axis_index("tile")
    seq_len = L
    w_half = lax.all_gather(weight.astype(jnp.bfloat16), "replica", axis=1, tiled=True)
    public_total = public_tokens.shape[0] * replicas
    block_x = public_tokens
    public_out = lax.psum_scatter(
        jnp.dot(block_x, w_half, preferred_element_type=jnp.float32),
        "tile",
        scatter_dimension=0,
        tiled=True,
    )
    public_delta = (public_out - public_targets.astype(jnp.float32)).astype(jnp.bfloat16)
    block_x = public_tokens
    public_grad = lax.dot_general(
        block_x,
        lax.all_gather(public_delta, "tile", axis=0, tiled=True),
        contract_rows,
        preferred_element_type=jnp.float32,
    )
    grad_owned = lax.psum_scatter(
        public_grad, "replica", scatter_dimension=1, tiled=True
    ) / math.sqrt(public_total)
    new_public = beta_public * public_moment + (1.0 - beta_public) * grad_owned * grad_owned
    precond_owned = 1.0 / (jnp.sqrt(new_public) + public_epsilon)
    precond = lax.all_gather(precond_owned, "replica", axis=1, tiled=True)
    counts_row = token_counts[0]
    slots_all = private_tokens.shape[0]
    slot_rows = private_targets.shape[0]
    block_x = private_tokens
    private_out = lax.psum_scatter(
        jnp.dot(block_x, w_half, preferred_element_type=jnp.float32),
        "tile",
        scatter_dimension=0,
        tiled=True,
    )
    local_live = live_slots(tile_pos * slot_rows, slot_rows, counts_row, seq_len)
    local_delta = jnp.where(
        local_live[:, None], private_out - private_targets.astype(jnp.float32), 0.0
    ).astype(jnp.bfloat16)
    private_delta = lax.all_gather(local_delta, "tile", axis=0, tiled=True)

    def example_norm(example):
        first_row = example * seq_len
        block_x = lax.dynamic_slice_in_dim(private_tokens, first_row, seq_len, 0)
        block_d = lax.dynamic_slice_in_dim(private_delta, first_row, seq_len, 0)
        grads = lax.dot_general(block_x, block_d, contract_rows, preferred_element_type=jnp.float32)
        scaled = grads * precond
        return jnp.sum(scaled * scaled)

    examples_here = token_counts.shape[1]
    partial_norms = lax.map(example_norm, jnp.arange(examples_here, dtype=jnp.int32))
    squares = lax.psum(partial_norms, "tile")
    clip_norm = clip_factor * math.sqrt(L * D * Q)
    factors = clip_norm / jnp.maximum(jnp.sqrt(squares), clip_norm)
    rows_at, owners = slot_owner(0, slots_all, seq_len)
    slot_factor = per_slot(owners, factors)
    weighted = (slot_factor[:, None] * private_delta.astype(jnp.float32)).astype(jnp.bfloat16)
    summed = precond * lax.dot_general(
        private_tokens, weighted, contract_rows, preferred_element_type=jnp.float32
    )
    summed_owned = lax.psum_scatter(summed, "replica", scatter_dimension=1, tiled=True)
    examples_total = examples_here * replicas
    noise_scale = noise_level * clip_factor * math.sqrt(L)
    gradient = (summed_owned + noise_scale * noise_draw) / examples_total
    new_first = beta_first * adam_first + (1.0 - beta_first) * gradient
    new_second = beta_second * adam_second + (1.0 - beta_second) * gradient * gradient
    first_hat = new_first / (1.0 - beta_first**2)
    second_hat = new_second / (1.0 - beta_second**2)
    new_weight = weight - learn_rate * first_hat / (jnp.sqrt(second_hat) + adam_epsilon)
    return (new_weight, new_first, new_second, new_public)


def solution(mesh):
    placed = (
        P("replica", "tile"),
        P(("replica", "tile"), None),
        P("replica", "tile"),
        P(("replica", "tile"), None),
        P("replica", None),
        P("tile", "replica"),
        P("tile", "replica"),
        P("tile", "replica"),
        P("tile", "replica"),
        P("tile", "replica"),
    )
    return jax.shard_map(
        on_device,
        mesh=mesh,
        in_specs=placed,
        out_specs=(
            P("tile", "replica"),
            P("tile", "replica"),
            P("tile", "replica"),
            P("tile", "replica"),
        ),
        check_vma=False,
    )
```

profile of v0, /device:TPU:0, one launch (start us, length us, event | category | flops | bytes accessed | tf_op | source)
XLA Modules:
  0.0 1037.2 jit_solution(3253973531232010438)
XLA Ops:
  7.2 3.0 convert_element_type.23
  10.3 0.0 reduce-scatter.5.cloned.1.call-start
  10.3 102.2 %all-gather.5.cloned.1.call-done = bf16[1280,4096]{1,0:T(8,128)(2,1)} async-done(((bf16[1280,512]{1,0:T(8,128)(2,1)}), bf16[1280,4096]{1,0:T(8,128)(2,1)}) %all-gather.5.cloned.1.call-update) | async-done | bytes 10485776 | tf_op jit(solution)/shard_map/all_gather | solution.py:54
  112.5 8.4 fusion.8
  120.9 0.0 all-gather.7.cloned.1.call-start
  121.0 51.2 %reduce-scatter.5.cloned.1.call-done = f32[64,4096]{1,0:T(8,128)} async-done(((f32[256,4096]{1,0:T(8,128)}), f32[64,4096]{1,0:T(8,128)}) %reduce-scatter.5.cloned.1.call-update) | async-done | bytes 1048592 | tf_op jit(solution)/shard_map/reduce_scatter | solution.py:57
  172.1 2.1 subtract_convert_fusion
  174.3 0.0 reduce-scatter.7.cloned.1.call-start
  174.3 35.7 %all-gather.7.cloned.1.call-done = bf16[256,4096]{1,0:T(8,128)(2,1)} async-done(((bf16[64,4096]{1,0:T(8,128)(2,1)}), bf16[256,4096]{1,0:T(8,128)(2,1)}) %all-gather.7.cloned.1.call-update) | async-done | bytes 2097168 | tf_op jit(solution)/shard_map/all_gather | solution.py:67
  210.0 11.5 %convolution_bitcast_fusion = f32[1280,4096]{0,1:T(8,128)} fusion(bf16[256,4096]{1,0:T(8,128)(2,1)} %all-gather.7.cloned.1.call-done, bf16[256,1280]{1,0:T(8,128)(2,1)S(1)} %copy-done), kind=kOutput, calls=%fused_computation.5 | convolution fusion | flops 2684354560 | bytes 23724032 | tf_op jit(solution)/shard_map/dot_general | solution.py:65
  221.6 0.0 reduce-scatter.9.cloned.1.call-start
  221.7 1.1 copy-done.2
  222.8 10.1 fusion.9
  233.0 1.7 copy-done.3
  234.7 2.1 copy.25
  236.7 192.7 %reduce-scatter.7.cloned.1.call-done = f32[1280,512]{0,1:T(8,128)} async-done(((f32[1280,4096]{0,1:T(8,128)}), f32[1280,512]{0,1:T(8,128)}) %reduce-scatter.7.cloned.1.call-update) | async-done | bytes 2621456 | tf_op jit(solution)/shard_map/reduce_scatter | solution.py:71
  429.5 5.2 add_divide_fusion
  434.8 0.6 copy-done.6
  435.3 0.1 select_reduce_fusion.1
  435.4 65.7 %reduce-scatter.9.cloned.1.call-done = f32[96,4096]{1,0:T(8,128)} async-done(((f32[384,4096]{1,0:T(8,128)}), f32[96,4096]{1,0:T(8,128)}) %reduce-scatter.9.cloned.1.call-update) | async-done | bytes 1572880 | tf_op jit(solution)/shard_map/reduce_scatter | solution.py:81
  501.2 2.5 select_convert_fusion
  503.7 0.2 reduce-scatter.11.cloned.1.call-start
  504.0 184.9 %all-gather.9.cloned.1.call-done = f32[1280,4096]{0,1:T(8,128)} async-done(((f32[1280,512]{0,1:T(8,128)}), f32[1280,4096]{0,1:T(8,128)}) %all-gather.9.cloned.1.call-update) | async-done | bytes 20971536 | tf_op jit(solution)/shard_map/all_gather | solution.py:76
  688.8 22.6 %copy.26 = f32[1280,4096]{1,0:T(8,128)} copy(f32[1280,4096]{0,1:T(8,128)} %all-gather.9.cloned.1.call-done) | data formatting | bytes 41943040 | tf_op jit(solution)/shard_map/while | solution.py:102
  711.4 22.2 %all-gather.11.cloned.1.call-done = bf16[384,4096]{1,0:T(8,128)(2,1)} async-done(((bf16[96,4096]{1,0:T(8,128)(2,1)}), bf16[384,4096]{1,0:T(8,128)(2,1)}) %all-gather.11.cloned.1.call-update) | async-done | bytes 3145744 | tf_op jit(solution)/shard_map/all_gather | solution.py:91
  733.6 46.9 %while.10 = (s32[]{:T(128)}, f32[3]{0:T(128)S(1)}, s32[3]{0:T(128)S(1)}, bf16[384,1280]{1,0:T(8,128)(2,1)}, bf16[384,4096]{1,0:T(8,128)(2,1)}, /*index=5*/f32[12...) while((s32[]{:T(128)}, f32[3]{0:T(128)S(1)}, s32[3]{0:T(128)S(1)}, ...), condition=%wide.region_6.7_spmd, body=%wide.region_4.6_spmd.sunk | while | flops 1357905920 | bytes 22348976 | solution.py:102
  733.6 0.6 dynamic_slice.19
  734.8 13.6 %multiply_reduce_fusion.2 = f32[]{:T(128)} fusion(f32[1280,4096]{1,0:T(8,128)} %get-tuple-element.136, bf16[384,4096]{1,0:T(8,128)(2,1)} %get-tuple-element.135, s32[]{:T(128)S(6)} %select_n.60, bf16[384,1280]{1,0:T(8,128)(2,1)} %get-tuple-element.134), kind=kOutput, calls=%fused_computation.clone.1 | convolution fusion | flops 1357905920 | bytes 22348804 | tf_op jit(solution)/shard_map/while/body/eval_jaxpr/dot_general | solution.py:97
  748.5 0.8 dynamic_update_slice.5
  749.2 0.6 dynamic_slice.19
  750.5 13.6 %multiply_reduce_fusion.2 = f32[]{:T(128)} fusion(f32[1280,4096]{1,0:T(8,128)} %get-tuple-element.136, bf16[384,4096]{1,0:T(8,128)(2,1)} %get-tuple-element.135, s32[]{:T(128)S(6)} %select_n.60, bf16[384,1280]{1,0:T(8,128)(2,1)} %get-tuple-element.134), kind=kOutput, calls=%fused_computation.clone.1 | convolution fusion | flops 1357905920 | bytes 22348804 | tf_op jit(solution)/shard_map/while/body/eval_jaxpr/dot_general | solution.py:97
  764.1 0.8 dynamic_update_slice.5
  764.8 0.6 dynamic_slice.19
  766.1 13.6 %multiply_reduce_fusion.2 = f32[]{:T(128)} fusion(f32[1280,4096]{1,0:T(8,128)} %get-tuple-element.136, bf16[384,4096]{1,0:T(8,128)(2,1)} %get-tuple-element.135, s32[]{:T(128)S(6)} %select_n.60, bf16[384,1280]{1,0:T(8,128)(2,1)} %get-tuple-element.134), kind=kOutput, calls=%fused_computation.clone.1 | convolution fusion | flops 1357905920 | bytes 22348804 | tf_op jit(solution)/shard_map/while/body/eval_jaxpr/dot_general | solution.py:97
  779.7 0.8 dynamic_update_slice.5
  780.5 9.1 psum.7
  789.6 0.1 select_reduce_fusion
  789.7 15.0 %bitcast_multiply_fusion = f32[1280,4096]{0,1:T(8,128)} fusion(f32[1280,4096]{0,1:T(8,128)} %all-gather.9.cloned.1.call-done, bf16[384,1280]{1,0:T(8,128)(2,1)} %get-tuple-element.158, bf16[384,4096]{1,0:T(8,128)(2,1)} %get-tuple-element.155, f32[384]{0:T(512)S(1)} %select_reduce_fusion), kind=kOutput, calls=%fused_computation.4 | convolution fusion | flops 4036493312 | bytes 46073344 | tf_op jit(solution)/shard_map/dot_general | solution.py:109
  804.8 3.2 copy.29
  808.0 3.3 copy.24
  811.3 3.4 copy.27
  814.7 3.2 copy.28
  818.0 2.1 copy.33
  820.0 192.6 %reduce-scatter.11.cloned.1.call-done = f32[1280,512]{0,1:T(8,128)} async-done(((f32[1280,4096]{0,1:T(8,128)}), f32[1280,512]{0,1:T(8,128)}) %reduce-scatter.11.cloned.1.call-update) | async-done | bytes 2621456 | tf_op jit(solution)/shard_map/reduce_scatter | solution.py:112
  1012.6 9.1 divide_subtract_fusion
  1021.7 3.2 copy.30
  1025.0 2.1 copy.31
  1027.0 3.3 copy.32
  (28 shorter events, 0.3 us)
Async XLA Ops:
  7.2 105.4 %copy-start = (bf16[256,1280]{1,0:T(8,128)(2,1)S(1)}, bf16[256,1280]{1,0:T(8,128)(2,1)}, u32[]{:S(2)}) copy-start(bf16[256,1280]{1,0:T(8,128)(2,1)} %param.12) | copy-start | bytes 1966084
  7.2 105.3 %all-gather.5.cloned.1.call-start = ((), (), s32[]{:S(2)}) async-start(), calls=%async_computation.4 | async-start | bytes 11796480 | tf_op jit(solution)/shard_map/all_gather | solution.py:54
  10.3 161.9 %reduce-scatter.5.cloned.1.call-start = ((), (), s32[]{:S(2)}) async-start(), calls=%async_computation.5 | async-start | bytes 5242880 | tf_op jit(solution)/shard_map/reduce_scatter | solution.py:57
  120.9 51.2 %copy-start.5 = (bf16[64,4096]{1,0:T(8,128)(2,1)S(1)}, bf16[64,4096]{1,0:T(8,128)(2,1)}, u32[]{:S(2)}) copy-start(bf16[64,4096]{1,0:T(8,128)(2,1)} %param.13) | copy-start | bytes 1572868
  120.9 89.1 %all-gather.7.cloned.1.call-start = ((), (), s32[]{:S(2)}) async-start(), calls=%async_computation.6 | async-start | bytes 2621440 | tf_op jit(solution)/shard_map/all_gather | solution.py:67
  174.3 255.2 %reduce-scatter.7.cloned.1.call-start = ((), (), s32[]{:S(2)}) async-start(), calls=%async_computation.7 | async-start | bytes 23592960 | tf_op jit(solution)/shard_map/reduce_scatter | solution.py:71
  221.6 1.2 copy-start.2
  221.6 279.6 %reduce-scatter.9.cloned.1.call-start = ((), (), s32[]{:S(2)}) async-start(), calls=%async_computation.9 | async-start | bytes 7864320 | tf_op jit(solution)/shard_map/reduce_scatter | solution.py:81
  232.9 1.7 copy-start.3
  233.0 455.9 %all-gather.9.cloned.1.call-start = ((), (), s32[]{:S(2)}) async-start(), calls=%async_computation.8 | async-start | bytes 23592960 | tf_op jit(solution)/shard_map/all_gather | solution.py:76
  434.7 0.7 copy-start.6
  434.7 66.5 %copy-start.4 = (bf16[96,4096]{1,0:T(8,128)(2,1)S(1)}, bf16[96,4096]{1,0:T(8,128)(2,1)}, u32[]{:S(2)}) copy-start(bf16[96,4096]{1,0:T(8,128)(2,1)} %param.15) | copy-start | bytes 2359300
  434.7 298.9 %all-gather.11.cloned.1.call-start = ((), (), s32[]{:S(2)}) async-start(), calls=%async_computation.10 | async-start | bytes 3932160 | tf_op jit(solution)/shard_map/all_gather | solution.py:91
  503.7 508.9 %reduce-scatter.11.cloned.1.call-start = ((), (), s32[]{:S(2)}) async-start(), calls=%async_computation.11 | async-start | bytes 23592960 | tf_op jit(solution)/shard_map/reduce_scatter | solution.py:112
  1027.0 3.3 copy-start.1
Sparse Core Ops, SparseCore 0:
  10.4 102.0 all-gather.4
  121.1 51.0 reduce-scatter.4
  174.7 35.2 all-gather.6
  221.7 207.6 reduce-scatter.6
  432.6 68.5 reduce-scatter.8
  503.3 185.4 all-gather.8
  691.4 42.1 all-gather.10
  804.9 207.6 reduce-scatter.10
where the time goes:
time: 1040 us
  waiting for transfers between devices  847 us (81%)
  matrix products  86 us (8%)
  local copies, waits for them, and re-layouts  55.9 us (5%)
  other arithmetic  22.2 us (2%)
  between operations  14.2 us (1%)
    reduce_scatter x1, waiting for transfers between devices, on_device(): lax.psum_scatter(public_grad, 'replica', scatter_dimension=1, tiled=True)  193 us
    reduce_scatter x1, waiting for transfers between devices, on_device(): lax.psum_scatter(summed, 'replica', scatter_dimension=1, tiled=True)  193 us
    all_gather x1, waiting for transfers between devices, on_device(): precond = lax.all_gather(precond_owned, 'replica', axis=1, tiled=True)  185 us
    reduce_scatter x2, waiting for transfers between devices, on_device(): lax.psum_scatter(jnp.dot(block_x, w_half, preferred_element_type=jnp.floa...  117 us
    all_gather x1, waiting for transfers between devices, on_device(): lax.all_gather(weight.astype(jnp.bfloat16), 'replica', axis=1, tiled=True)  102 us
    dot_general x3, matrix products, example_norm(): lax.dot_general(block_x, block_d, contract_rows, preferred_element_type=j...  40.9 us
    all_gather x1, waiting for transfers between devices, on_device(): lax.all_gather(public_delta, 'tile', axis=0, tiled=True)  35.7 us
    unnamed x23, local copies, waits for them, and re-layouts  29.3 us
  transfers between devices with their start and end apart: 8, of which 8 were waited for; matrix products, arithmetic and copies ran while one was open for 6% of the time, Pallas kernels for 0%

commit v1 on v0

v1 whole, which is shorter than its diff:
```python
import math

import jax
import jax.numpy as jnp
from jax import lax
from jax.experimental import pallas as pl
from jax.experimental.pallas import tpu as pltpu
from jax.sharding import PartitionSpec as P

beta_first = 0.9
beta_second = 0.99
beta_public = 0.9
public_epsilon = 0.001
adam_epsilon = 1e-08
clip_factor = 0.6
noise_level = 4.0
learn_rate = 0.01
contract_rows = (((0,), (0,)), ((), ()))


def swap(value, bit):
    size = lax.axis_size("tile")
    return lax.ppermute(value, "tile", [(i, i ^ bit) for i in range(size)])


def bits_of(size, backwards):
    order = [1 << k for k in range(size.bit_length() - 1)]
    return order[::-1] if backwards else order


def sum_to_owner(value, backwards):
    size = lax.axis_size("tile")
    me = lax.axis_index("tile")
    groups, _, rows, cols = value.shape
    order = bits_of(size, backwards)
    names = [1 << k for k in range(size.bit_length() - 1)][::-1]
    value = value.reshape((groups,) + (2,) * len(names) + (rows, cols))
    for bit in order:
        axis = 1 + names.index(bit)
        names.remove(bit)
        mine = (me // bit) % 2
        away = lax.dynamic_index_in_dim(value, 1 - mine, axis, keepdims=False)
        kept = lax.dynamic_index_in_dim(value, mine, axis, keepdims=False)
        value = kept + swap(away.astype(jnp.bfloat16), bit).astype(jnp.float32)
    return value


def gather_tiles(value, backwards):
    size = lax.axis_size("tile")
    me = lax.axis_index("tile")
    groups, rows, cols = value.shape
    names = []
    for bit in bits_of(size, backwards):
        mine = (me // bit) % 2
        other = swap(value, bit)
        names = sorted(names + [bit], reverse=True)
        axis = 1 + names.index(bit)
        low = jnp.where(mine == 0, value, other)
        high = jnp.where(mine == 0, other, value)
        value = jnp.stack([low, high], axis=axis)
    return value.reshape(groups, size, rows, cols)


def norm_kernel(x_ref, d_ref, p_ref, out_ref):
    total = jnp.zeros(out_ref.shape[1:], jnp.float32)
    rows = x_ref.shape[1]
    step = 256 if rows % 256 == 0 else 64
    for at in range(0, rows, step):
        grads = lax.dot_general(
            x_ref[:, at : at + step], d_ref[...], contract_rows, preferred_element_type=jnp.float32
        )
        scaled = grads * p_ref[at : at + step, :]
        total += jnp.sum((scaled * scaled).reshape(step // 8, 8, -1), axis=0)
    out_ref[0] = total


def example_squares(tokens, delta, precond, examples):
    slots, rows = tokens.shape
    seq_len = slots // examples
    cols = delta.shape[1]
    parts = pl.pallas_call(
        norm_kernel,
        grid=(examples,),
        in_specs=[
            pl.BlockSpec((seq_len, rows), lambda j: (j, 0)),
            pl.BlockSpec((seq_len, cols), lambda j: (j, 0)),
            pl.BlockSpec((rows, cols), lambda j: (0, 0)),
        ],
        out_specs=pl.BlockSpec((1, 8, cols), lambda j: (j, 0, 0)),
        out_shape=jax.ShapeDtypeStruct((examples, 8, cols), jnp.float32),
        compiler_params=pltpu.CompilerParams(vmem_limit_bytes=40 * 1024 * 1024),
        cost_estimate=pl.CostEstimate(
            flops=2 * slots * rows * cols, bytes_accessed=2 * slots * (rows + cols), transcendentals=0
        ),
        name="example_norms",
    )(tokens, delta, precond)
    return jnp.sum(parts, axis=(1, 2))


def errors_of(tokens, weight, targets, replicas, pieces):
    size = lax.axis_size("tile")
    cols = weight.shape[1]
    span = tokens.shape[0] // replicas
    per = replicas // pieces
    found = []
    for piece in range(pieces):
        block = tokens[piece * per * span : (piece + 1) * per * span]
        out = jnp.dot(block, weight, preferred_element_type=jnp.float32)
        out = sum_to_owner(out.reshape(per, size, span // size, cols), piece % 2 == 1)
        aims = targets[piece * per : (piece + 1) * per].astype(jnp.float32)
        delta = (out - aims).astype(jnp.bfloat16)
        found.append(gather_tiles(delta, piece % 2 == 1).reshape(per * span, cols))
    return jnp.concatenate(found, axis=0)


def on_device(
    public_tokens,
    public_targets,
    private_tokens,
    private_targets,
    token_counts,
    weight,
    public_moment,
    adam_first,
    adam_second,
    noise_draw,
):
    replicas = lax.axis_size("replica")
    tiles = lax.axis_size("tile")
    replica = lax.axis_index("replica")
    examples_here = token_counts.shape[1]
    examples_total = examples_here * replicas
    slots_here = private_tokens.shape[0]
    seq_len = slots_here // examples_here
    width = weight.shape[0] * tiles
    columns = weight.shape[1] * replicas
    cols = weight.shape[1]
    public_total = public_tokens.shape[0] * replicas

    limits = jnp.repeat(token_counts[0], seq_len, total_repeat_length=slots_here)
    live = jnp.arange(slots_here, dtype=jnp.int32) % seq_len < limits
    private_tokens = jnp.where(live[:, None], private_tokens, jnp.zeros((), private_tokens.dtype))

    w_half = weight.astype(jnp.bfloat16)
    aims = jnp.concatenate([public_targets, private_targets], axis=0)
    aims = lax.all_to_all(aims, "replica", split_axis=1, concat_axis=0, tiled=True)
    aims = aims.reshape(replicas, -1, cols)
    public_aims = aims[:, : public_targets.shape[0]]
    private_aims = aims[:, public_targets.shape[0] :]

    public_all = lax.all_gather(public_tokens, "replica", axis=0, tiled=True)
    private_all = lax.all_gather(private_tokens, "replica", axis=0, tiled=True)

    public_delta = errors_of(public_all, w_half, public_aims, replicas, 2)
    public_grad = lax.dot_general(
        public_all, public_delta, contract_rows, preferred_element_type=jnp.float32
    ) / math.sqrt(public_total)
    new_public = beta_public * public_moment + (1.0 - beta_public) * public_grad * public_grad
    precond = 1.0 / (jnp.sqrt(new_public) + public_epsilon)

    private_delta = errors_of(private_all, w_half, private_aims, replicas, 2)
    squares = example_squares(private_all, private_delta, precond, examples_total)
    squares = lax.psum(squares, ("replica", "tile"))
    clip_norm = clip_factor * math.sqrt(seq_len * width * columns)
    factors = clip_norm / jnp.maximum(jnp.sqrt(squares), clip_norm)
    slot_factor = jnp.repeat(factors, seq_len, total_repeat_length=slots_here * replicas)
    weighted = (slot_factor[:, None] * private_delta.astype(jnp.float32)).astype(jnp.bfloat16)
    summed = precond * lax.dot_general(
        private_all, weighted, contract_rows, preferred_element_type=jnp.float32
    )
    noise_scale = noise_level * clip_factor * math.sqrt(seq_len)
    gradient = (summed + noise_scale * noise_draw) / examples_total
    new_first = beta_first * adam_first + (1.0 - beta_first) * gradient
    new_second = beta_second * adam_second + (1.0 - beta_second) * gradient * gradient
    first_hat = new_first / (1.0 - beta_first**2)
    second_hat = new_second / (1.0 - beta_second**2)
    new_weight = weight - learn_rate * first_hat / (jnp.sqrt(second_hat) + adam_epsilon)
    return (new_weight, new_first, new_second, new_public)


def solution(mesh):
    placed = (
        P("replica", "tile"),
        P(("replica", "tile"), None),
        P("replica", "tile"),
        P(("replica", "tile"), None),
        P("replica", None),
        P("tile", "replica"),
        P("tile", "replica"),
        P("tile", "replica"),
        P("tile", "replica"),
        P("tile", "replica"),
    )
    return jax.shard_map(
        on_device,
        mesh=mesh,
        in_specs=placed,
        out_specs=(
            P("tile", "replica"),
            P("tile", "replica"),
            P("tile", "replica"),
            P("tile", "replica"),
        ),
        check_vma=False,
    )
```

time: 1040 us -> 344 us (0.33)
  waiting for transfers between devices: 847 us -> 181 us
  matrix products: 86 us -> 33.4 us
  local copies, waits for them, and re-layouts: 55.9 us -> 8.86 us
  blocking collectives: 9.12 us -> 38.1 us
  starting transfers between devices: 0.51 us -> 23.7 us
  Pallas kernels: 0 us -> 12.8 us
    reduce_scatter x4 -> x0, waiting for transfers between devices: 502 us -> none  [the longest x1 193 us: on_device(): lax.psum_scatter(public_grad, 'replica', scatter_dimension=1, tiled=True)]
    all_gather x4 -> x2, waiting for transfers between devices: 345 us -> 109 us  [the longest x1 72.8 us: on_device(): public_all = lax.all_gather(public_tokens, 'replica', axis=0, tiled=True)]
    ppermute x0 -> x16, waiting for transfers between devices: none -> 72.3 us  [swap(): return lax.ppermute(value, 'tile', [(i, i ^ bit) for i in range(size)])]
    dot_general x7 -> x6, matrix products: 86 us -> 33.4 us  [the longest x1 15.9 us: on_device(): lax.dot_general(private_all, weighted, contract_rows, preferred_element_t...]
    psum x1, blocking collectives: 9.12 us -> 38.1 us  [on_device(): squares = lax.psum(squares, ('replica', 'tile'))]
    unnamed x23 -> x26, local copies, waits for them, and re-layouts: 29.3 us -> 2.6 us
    while x1 -> x0, local copies, waits for them, and re-layouts: 22.6 us -> none  [on_device(): lax.map(example_norm, jnp.arange(examples_here, dtype=jnp.int32))]
    ppermute x0 -> x16, starting transfers between devices: none -> 17.3 us  [swap(): return lax.ppermute(value, 'tile', [(i, i ^ bit) for i in range(size)])]
  transfers between devices with their start and end apart: 8 -> 19, of which waited for: 8 -> 15; matrix products, arithmetic and copies ran while one was open for 6% -> 11% of each run, Pallas kernels for 0% -> 0%
where the time goes in v1:
time: 344 us
  waiting for transfers between devices  181 us (53%)
  blocking collectives  38.1 us (11%)
  matrix products  33.4 us (10%)
  other arithmetic  30.7 us (9%)
  starting transfers between devices  23.7 us (7%)
  between operations  14.4 us (4%)
  Pallas kernels  12.8 us (4%)
  local copies, waits for them, and re-layouts  8.86 us (3%)
    all_gather x1, waiting for transfers between devices, on_device(): public_all = lax.all_gather(public_tokens, 'replica', axis=0, tiled=True)  72.8 us
    ppermute x16, waiting for transfers between devices, swap(): return lax.ppermute(value, 'tile', [(i, i ^ bit) for i in range(size)])  72.3 us
    psum x1, blocking collectives, on_device(): squares = lax.psum(squares, ('replica', 'tile'))  38.1 us
    all_gather x1, waiting for transfers between devices, on_device(): private_all = lax.all_gather(private_tokens, 'replica', axis=0, tiled=True)  35.7 us
    ppermute x16, starting transfers between devices, swap(): return lax.ppermute(value, 'tile', [(i, i ^ bit) for i in range(size)])  17.3 us
    dot_general x1, matrix products, on_device(): lax.dot_general(private_all, weighted, contract_rows, preferred_element_t...  15.9 us
    pallas_call x1, Pallas kernels, example_squares(): pl.pallas_call(norm_kernel, grid=(examples,), in_specs=[pl.BlockSpec((seq...  12.8 us
    dot_general x4, matrix products, errors_of(): out = jnp.dot(block, weight, preferred_element_type=jnp.float32)  12 us
  transfers between devices with their start and end apart: 19, of which 15 were waited for; matrix products, arithmetic and copies ran while one was open for 11% of the time, Pallas kernels for 0%

profile of v1, /device:TPU:0, one launch (start us, length us, event | category | flops | bytes accessed | tf_op | source)
XLA Modules:
  0.0 343.5 jit_solution(10737314313757655740)
XLA Ops:
  7.2 0.7 all-gather.3.cloned.1.call-update
  8.0 1.4 fusion.46
  9.3 2.0 fusion.42
  11.3 2.3 broadcast_select_fusion
  13.8 1.2 copy.100
  15.0 6.3 %all-to-all-start = ((bf16[160,8,512]{2,0,1:T(8,128)(2,1)}), bf16[160,8,512]{2,0,1:T(8,128)(2,1)S(1)}, u32[]{:S(2)}, u32[]{:S(2)}) async-start(bf16[160,8,512]{2,0,1:T(8,128)(2,1)} %bitcast.162), calls=%async_computation | async-start | bytes 2621440 | tf_op jit(solution)/shard_map/all_to_all | solution.py:146
  21.3 1.9 convert_element_type.105
  23.3 72.8 %all-gather.3.cloned.1.call-done = bf16[2048,1280]{1,0:T(8,128)(2,1)} async-done(((bf16[256,1280]{1,0:T(8,128)(2,1)}), bf16[2048,1280]{1,0:T(8,128)(2,1)}) %all-gather.3.cloned.1.call-update) | async-done | bytes 5242896 | tf_op jit(solution)/shard_map/all_gather | solution.py:151
  96.1 3.4 fusion.6
  99.6 1.2 copy-done.5
  100.8 1.5 collective-permute-start.4
  102.3 1.5 fusion.8
  103.8 1.3 copy-done.3
  105.2 1.5 collective-permute-start
  106.7 8.3 %collective-permute-done.4 = bf16[4,2,64,512]{3,2,0,1:T(8,128)(2,1)} collective-permute-done((bf16[4,2,64,512]{3,2,0,1:T(8,128)(2,1)S(1)}, bf16[4,2,64,512]{3,2,0,1:T(8,128)(2,1)}, u32[]{:S(2)}, u32[]{:S(2)}) %collective-permute-start.4) | collective-permute-done | bytes 524320 | tf_op jit(solution)/shard_map/ppermute | solution.py:23
  115.0 1.6 bitcast_add_fusion.3
  116.6 0.7 fusion.31
  117.3 1.5 collective-permute-start.5
  119.2 1.2 bitcast_add_fusion.4
  120.4 0.7 fusion.30
  121.1 1.1 collective-permute-start.1
  122.3 3.0 collective-permute-done.5
  125.3 3.5 %collective-permute-done.1 = bf16[4,64,512]{2,1,0:T(8,128)(2,1)} collective-permute-done((bf16[4,64,512]{2,1,0:T(8,128)(2,1)}, bf16[4,64,512]{2,1,0:T(8,128)(2,1)}, u32[]{:S(2)}, u32[]{:S(2)}) %collective-permute-start.1) | collective-permute-done | bytes 262176 | tf_op jit(solution)/shard_map/ppermute | solution.py:23
  128.8 2.0 fusion.27
  130.8 1.5 collective-permute-start.2
  132.8 4.6 %collective-permute-done.2 = bf16[4,64,512]{2,1,0:T(8,128)(2,1)S(1)} collective-permute-done((bf16[4,64,512]{2,1,0:T(8,128)(2,1)}, bf16[4,64,512]{2,1,0:T(8,128)(2,1)S(1)}, u32[]{:S(2)}, u32[]{:S(2)}) %collective-permute-start.2) | collective-permute-done | bytes 262176 | tf_op jit(solution)/shard_map/ppermute | solution.py:23
  137.4 1.0 select_bitcast_fusion.15
  138.4 35.7 %all-gather.5.cloned.1.call-done.x_ref = bf16[3072,1280]{1,0:T(8,128)(2,1)} async-done(((bf16[384,1280]{1,0:T(8,128)(2,1)}), bf16[3072,1280]{1,0:T(8,128)(2,1)}) %all-gather.5.cloned.1.call-update) | async-done | bytes 7864336 | tf_op jit(solution)/shard_map/all_gather | solution.py:152
  174.1 4.8 %fusion = f32[1536,512]{1,0:T(8,128)S(1)} fusion(bf16[1280,512]{1,0:T(8,128)(2,1)} %copy-done.1, bf16[3072,1280]{1,0:T(8,128)(2,1)} %all-gather.5.cloned.1.call-done.x_ref), kind=kOutput, calls=%fused_computation.1 | convolution fusion | flops 2013265920 | bytes 8388608 | tf_op jit(solution)/shard_map/dot_general | solution.py:108
  179.1 1.6 collective-permute-start.12
  180.7 2.2 fusion.2
  183.0 1.5 collective-permute-start.8
  185.9 13.6 %collective-permute-done.12 = bf16[4,2,96,512]{3,2,0,1:T(8,128)(2,1)S(1)} collective-permute-done((bf16[4,2,96,512]{3,2,0,1:T(8,128)(2,1)S(1)}, bf16[4,2,96,512]{3,2,0,1:T(8,128)(2,1)S(1)}, u32[]{:S(2)}, u32[]{:S(2)}) %collective-permute-start.12) | collective-permute-done | bytes 786464 | tf_op jit(solution)/shard_map/ppermute | solution.py:23
  199.9 1.6 collective-permute-start.13
  201.5 2.0 collective-permute-done.8
  204.4 10.3 %collective-permute-done.7 = bf16[4,2,64,512]{3,2,0,1:T(8,128)(2,1)S(1)} collective-permute-done((bf16[4,2,64,512]{3,2,0,1:T(8,128)(2,1)S(1)}, bf16[4,2,64,512]{3,2,0,1:T(8,128)(2,1)S(1)}, u32[]{:S(2)}, u32[]{:S(2)}) %collective-permute-start.7) | collective-permute-done | bytes 524320 | tf_op jit(solution)/shard_map/ppermute | solution.py:23
  215.0 7.2 %collective-permute-done.13 = bf16[4,96,512]{2,1,0:T(8,128)(2,1)S(1)} collective-permute-done((bf16[4,96,512]{2,1,0:T(8,128)(2,1)S(1)}, bf16[4,96,512]{2,1,0:T(8,128)(2,1)S(1)}, u32[]{:S(2)}, u32[]{:S(2)}) %collective-permute-start.13) | collective-permute-done | bytes 393248 | tf_op jit(solution)/shard_map/ppermute | solution.py:23
  222.5 1.5 collective-permute-start.10
  224.8 7.9 %collective-permute-done.10 = bf16[4,96,512]{2,1,0:T(8,128)(2,1)S(1)} collective-permute-done((bf16[4,96,512]{2,1,0:T(8,128)(2,1)S(1)}, bf16[4,96,512]{2,1,0:T(8,128)(2,1)S(1)}, u32[]{:S(2)}, u32[]{:S(2)}) %collective-permute-start.10) | collective-permute-done | bytes 393248 | tf_op jit(solution)/shard_map/ppermute | solution.py:23
  233.4 1.1 collective-permute-done.14
  235.1 5.5 %add_divide_fusion = (f32[1280,512]{1,0:T(8,128)S(1)}, f32[1280,512]{1,0:T(8,128)}) fusion(bf16[2048,1280]{1,0:T(8,128)(2,1)S(1)} %bitcast.184, bf16[1024,512]{1,0:T(8,128)(2,1)S(1)} %bitcast.178, bf16[1024,512]{1,0:T(8,128)(2,1)S(1)} %bitcast.179, f32[1280,512]{1,0:T(8,128)S(1)} %copy-done.10), kind=kOutput, calls=%fused_computation.17 | convolution fusion | flops 2693136384 | bytes 15204352 | tf_op jit(solution)/shard_map/dot_general | solution.py:155
  240.7 10.3 %collective-permute-done.11 = bf16[4,2,96,512]{3,2,0,1:T(8,128)(2,1)S(1)} collective-permute-done((bf16[4,2,96,512]{3,2,0,1:T(8,128)(2,1)S(1)}, bf16[4,2,96,512]{3,2,0,1:T(8,128)(2,1)S(1)}, u32[]{:S(2)}, u32[]{:S(2)}) %collective-permute-start.11) | collective-permute-done | bytes 786464 | tf_op jit(solution)/shard_map/ppermute | solution.py:23
  252.3 12.8 %example_norms.1 = f32[24,8,512]{2,1,0:T(8,128)S(1)} custom-call(bf16[3072,1280]{1,0:T(8,128)(2,1)S(1)} %copy-done, bf16[3072,512]{1,0:T(8,128)(2,1)S(1)} %pad_maximum_fusion.d_ref, f32[1280,512]{1,0:T(8,128)S(1)} %get-tuple-element.97.p_ref), custom_call_target="tpu_custom_call" | custom-call | flops 4026531840 | bytes 11010048 | tf_op jit(solution)/shard_map/example_norms/pallas_call | solution.py:81
  265.4 38.1 %psum.7 = f32[24]{0:T(128)S(1)} all-reduce(f32[24]{0:T(128)S(1)} %reduce_sum.9), channel_id=1, replica_groups=mesh['replica'=8,'tile'=4] {'replica','tile'}, use_global_device_ids=true, to_apply=%region_1.2 | all-reduce | flops 24 | bytes 192 | tf_op jit(solution)/shard_map/psum | solution.py:163
  303.5 0.7 fusion.44
  304.9 4.5 %compare_select_fusion.1 = (f32[3072,1]{0,1:T(1,128)S(1)}, s32[3072,1]{0,1:T(1,128)S(1)}) fusion(f32[]{:T(128)} %bitcast.70, f32[]{:T(128)} %bitcast.71, f32[]{:T(128)} %bitcast.72, f32[]{:T(128)} %bitcast.73, f32[]{:T(128)} %bitcast.74, f32[]{:T(128)} %bitcast.76, f32[]{:T(128)} %bitcast.75, s32[3072,1]{0,1:T(1,128)S(1)} %bitcast.181, ...), kind=kLoop, calls=%fused_computation.99 | loop fusion | flops 43008 | bytes 49180 | tf_op jit(solution)/shard_map/jit(_take)/gather | solution.py:166
  309.9 10.8 %select_select_fusion = f32[3072]{0:T(1024)S(1)} fusion(pred[3072]{0:T(1024)(128)(4,1)S(1)} %get-tuple-element.44, pred[3072]{0:T(1024)(128)(4,1)S(1)} %get-tuple-element.43, pred[3072]{0:T(1024)(128)(4,1)S(1)} %get-tuple-element.42, pred[3072]{0:T(1024)(128)(4,1)S(1)} %get-tuple-element.41, pred[3072]{0:T(1024)(128)(4,1)S(1)} %get-tuple-element.40, ...), kind=kLoop, calls=%fused_computation.106 | loop fusion | flops 79872 | bytes 76868 | tf_op jit(solution)/shard_map/jit(_take)/select_n | solution.py:166
  320.7 15.9 %divide_subtract_fusion = (f32[1280,512]{1,0:T(8,128)}, f32[1280,512]{1,0:T(8,128)}, f32[1280,512]{1,0:T(8,128)}) fusion(f32[1280,512]{1,0:T(8,128)} %param.19, f32[1280,512]{1,0:T(8,128)} %param.21, f32[1280,512]{1,0:T(8,128)} %param.22, f32[1280,512]{1,0:T(8,128)} %param.23, bf16[3072,1280]{1,0:T(8,128)(2,1)} %all-gather.5.cloned.1.call-done.x_ref, ...), kind=kOutput, calls=%fused_computation.14 | convolution fusion | flops 4047765504 | bytes 31993856 | tf_op jit(solution)/shard_map/dot_general | solution.py:168
  (78 shorter events, 9.7 us)
Async XLA Ops:
  7.2 6.5 %copy-start.8 = (bf16[64,4096]{1,0:T(8,128)(2,1)S(1)}, bf16[64,4096]{1,0:T(8,128)(2,1)}, u32[]{:S(2)}) copy-start(bf16[64,4096]{1,0:T(8,128)(2,1)} %param.15) | copy-start | bytes 1572868
  7.2 6.5 %copy-start.7 = (bf16[96,4096]{1,0:T(8,128)(2,1)S(1)}, bf16[96,4096]{1,0:T(8,128)(2,1)}, u32[]{:S(2)}) copy-start(bf16[96,4096]{1,0:T(8,128)(2,1)} %param.17) | copy-start | bytes 2359300
  7.2 88.9 %all-gather.3.cloned.1.call-start = ((), (), s32[]{:S(2)}) async-start(), calls=%async_computation.1 | async-start | bytes 5898240 | tf_op jit(solution)/shard_map/all_gather | solution.py:151
  7.9 166.2 %all-gather.5.cloned.1.call-start = ((), (), s32[]{:S(2)}) async-start(), calls=%async_computation.2 | async-start | bytes 8847360 | tf_op jit(solution)/shard_map/all_gather | solution.py:152
  15.0 107.3 %all-to-all-start = ((bf16[160,8,512]{2,0,1:T(8,128)(2,1)}), bf16[160,8,512]{2,0,1:T(8,128)(2,1)S(1)}, u32[]{:S(2)}, u32[]{:S(2)}) async-start(bf16[160,8,512]{2,0,1:T(8,128)(2,1)} %bitcast.162), calls=%async_computation | async-start | bytes 2621440 | tf_op jit(solution)/shard_map/all_to_all | solution.py:146
  23.2 79.1 %copy-start.1 = (bf16[1280,512]{1,0:T(8,128)(2,1)}, bf16[1280,512]{1,0:T(8,128)(2,1)S(1)}, u32[]{:S(2)}) copy-start(bf16[1280,512]{1,0:T(8,128)(2,1)S(1)} %convert_element_type.105) | copy-start | bytes 3932164
  96.1 6.2 %copy-start.9 = (bf16[2048,1280]{1,0:T(8,128)(2,1)S(1)}, bf16[2048,1280]{1,0:T(8,128)(2,1)}, u32[]{:S(2)}) copy-start(bf16[2048,1280]{1,0:T(8,128)(2,1)} %all-gather.3.cloned.1.call-done) | copy-start | bytes 15728644
  99.5 1.3 copy-start.5
  100.8 14.2 %collective-permute-start.4 = (bf16[4,2,64,512]{3,2,0,1:T(8,128)(2,1)S(1)}, bf16[4,2,64,512]{3,2,0,1:T(8,128)(2,1)}, u32[]{:S(2)}, u32[]{:S(2)}) collective-permute-start(bf16[4,2,64,512]{3,2,0,1:T(8,128)(2,1)S(1)} %fusion.23), channel_id=1, source_target_pairs={{0,2},{1,3},{2,0},{3,1},{4,6},{5,7},{6,4},{7,5},{8,10},{9,11},{10,... | collective-permute-start | bytes 1572872 | tf_op jit(solution)/shard_map/ppermute | solution.py:23
  103.8 1.3 copy-start.3
  105.2 14.0 %collective-permute-start = (bf16[4,2,64,512]{3,2,0,1:T(8,128)(2,1)S(1)}, bf16[4,2,64,512]{3,2,0,1:T(8,128)(2,1)}, u32[]{:S(2)}, u32[]{:S(2)}) collective-permute-start(bf16[4,2,64,512]{3,2,0,1:T(8,128)(2,1)S(1)} %fusion.22), channel_id=1, source_target_pairs={{0,1},{1,0},{2,3},{3,2},{4,5},{5,4},{6,7},{7,6},{8,9},{9,8},{10,11... | collective-permute-start | bytes 1572872 | tf_op jit(solution)/shard_map/ppermute | solution.py:23
  106.7 12.4 %copy-start.4 = (f32[1024,512]{1,0:T(8,128)S(1)}, f32[1024,512]{1,0:T(8,128)}, u32[]{:S(2)}) copy-start(f32[1024,512]{1,0:T(8,128)} %copy-done.3) | copy-start | bytes 6291460
  117.3 8.0 %collective-permute-start.5 = (bf16[4,64,512]{2,1,0:T(8,128)(2,1)}, bf16[4,64,512]{2,1,0:T(8,128)(2,1)}, u32[]{:S(2)}, u32[]{:S(2)}) collective-permute-start(bf16[4,64,512]{2,1,0:T(8,128)(2,1)} %fusion.31), channel_id=1, source_target_pairs={{0,1},{1,0},{2,3},{3,2},{4,5},{5,4},{6,7},{7,6},{8,9},{9,8},{10,11... | collective-permute-start | bytes 786440 | tf_op jit(solution)/shard_map/ppermute | solution.py:23
  121.1 7.6 %collective-permute-start.1 = (bf16[4,64,512]{2,1,0:T(8,128)(2,1)}, bf16[4,64,512]{2,1,0:T(8,128)(2,1)}, u32[]{:S(2)}, u32[]{:S(2)}) collective-permute-start(bf16[4,64,512]{2,1,0:T(8,128)(2,1)} %fusion.30), channel_id=1, source_target_pairs={{0,2},{1,3},{2,0},{3,1},{4,6},{5,7},{6,4},{7,5},{8,10},{9,11},{10,... | collective-permute-start | bytes 786440 | tf_op jit(solution)/shard_map/ppermute | solution.py:23
  130.8 6.6 %collective-permute-start.2 = (bf16[4,64,512]{2,1,0:T(8,128)(2,1)}, bf16[4,64,512]{2,1,0:T(8,128)(2,1)S(1)}, u32[]{:S(2)}, u32[]{:S(2)}) collective-permute-start(bf16[4,64,512]{2,1,0:T(8,128)(2,1)} %get-tuple-element.54), channel_id=1, source_target_pairs={{0,1},{1,0},{2,3},{3,2},{4,5},{5,4},{6,7},{7,6},{8,9},{9,8},{10,11... | collective-permute-start | bytes 786440 | tf_op jit(solution)/shard_map/ppermute | solution.py:23
  132.3 52.9 %collective-permute-start.6 = (bf16[4,64,512]{2,1,0:T(8,128)(2,1)}, bf16[4,64,512]{2,1,0:T(8,128)(2,1)S(1)}, u32[]{:S(2)}, u32[]{:S(2)}) collective-permute-start(bf16[4,64,512]{2,1,0:T(8,128)(2,1)} %get-tuple-element.55), channel_id=1, source_target_pairs={{0,2},{1,3},{2,0},{3,1},{4,6},{5,7},{6,4},{7,5},{8,10},{9,11},{10,... | collective-permute-start | bytes 786440 | tf_op jit(solution)/shard_map/ppermute | solution.py:23
  138.4 42.2 %copy-start.2 = (bf16[1280,512]{1,0:T(8,128)(2,1)S(1)}, bf16[1280,512]{1,0:T(8,128)(2,1)}, u32[]{:S(2)}) copy-start(bf16[1280,512]{1,0:T(8,128)(2,1)} %copy-done.1) | copy-start | bytes 3932164
  174.1 6.6 %copy-start = (bf16[3072,1280]{1,0:T(8,128)(2,1)S(1)}, bf16[3072,1280]{1,0:T(8,128)(2,1)}, u32[]{:S(2)}) copy-start(bf16[3072,1280]{1,0:T(8,128)(2,1)} %all-gather.5.cloned.1.call-done.x_ref) | copy-start | bytes 23592964
  179.1 20.4 %collective-permute-start.12 = (bf16[4,2,96,512]{3,2,0,1:T(8,128)(2,1)S(1)}, bf16[4,2,96,512]{3,2,0,1:T(8,128)(2,1)S(1)}, u32[]{:S(2)}, u32[]{:S(2)}) collective-permute-start(bf16[4,2,96,512]{3,2,0,1:T(8,128)(2,1)S(1)} %fusion.17), channel_id=1, source_target_pairs={{0,2},{1,3},{2,0},{3,1},{4,6},{5,7},{6,4},{7,5},{8,10},{9,11},{10,... | collective-permute-start | bytes 2359304 | tf_op jit(solution)/shard_map/ppermute | solution.py:23
  182.9 2.3 copy-start.6
  183.0 20.5 %collective-permute-start.8 = (bf16[4,2,96,512]{3,2,0,1:T(8,128)(2,1)S(1)}, bf16[4,2,96,512]{3,2,0,1:T(8,128)(2,1)S(1)}, u32[]{:S(2)}, u32[]{:S(2)}) collective-permute-start(bf16[4,2,96,512]{3,2,0,1:T(8,128)(2,1)S(1)} %fusion.16), channel_id=1, source_target_pairs={{0,1},{1,0},{2,3},{3,2},{4,5},{5,4},{6,7},{7,6},{8,9},{9,8},{10,11... | collective-permute-start | bytes 2359304 | tf_op jit(solution)/shard_map/ppermute | solution.py:23
  184.6 39.4 %collective-permute-start.3 = (bf16[4,2,64,512]{3,2,1,0:T(8,128)(2,1)S(1)}, bf16[4,2,64,512]{3,2,1,0:T(8,128)(2,1)S(1)}, u32[]{:S(2)}, u32[]{:S(2)}) collective-permute-start(bf16[4,2,64,512]{3,2,1,0:T(8,128)(2,1)S(1)} %pad_maximum_fusion.8), channel_id=1, source_target_pairs={{0,2},{1,3},{2,0},{3,1},{4,6},{5,7},{6,4},{7,5},{8,10},{9,11},{10,... | collective-permute-start | bytes 1572872 | tf_op jit(solution)/shard_map/ppermute | solution.py:23
  185.3 29.4 %collective-permute-start.7 = (bf16[4,2,64,512]{3,2,0,1:T(8,128)(2,1)S(1)}, bf16[4,2,64,512]{3,2,0,1:T(8,128)(2,1)S(1)}, u32[]{:S(2)}, u32[]{:S(2)}) collective-permute-start(bf16[4,2,64,512]{3,2,0,1:T(8,128)(2,1)S(1)} %pad_maximum_fusion.9), channel_id=1, source_target_pairs={{0,1},{1,0},{2,3},{3,2},{4,5},{5,4},{6,7},{7,6},{8,9},{9,8},{10,11... | collective-permute-start | bytes 1572872 | tf_op jit(solution)/shard_map/ppermute | solution.py:23
  199.9 22.3 %collective-permute-start.13 = (bf16[4,96,512]{2,1,0:T(8,128)(2,1)S(1)}, bf16[4,96,512]{2,1,0:T(8,128)(2,1)S(1)}, u32[]{:S(2)}, u32[]{:S(2)}) collective-permute-start(bf16[4,96,512]{2,1,0:T(8,128)(2,1)S(1)} %fusion.29), channel_id=1, source_target_pairs={{0,1},{1,0},{2,3},{3,2},{4,5},{5,4},{6,7},{7,6},{8,9},{9,8},{10,11... | collective-permute-start | bytes 1179656 | tf_op jit(solution)/shard_map/ppermute | solution.py:23
  203.8 18.3 %collective-permute-start.9 = (bf16[4,96,512]{2,1,0:T(8,128)(2,1)S(1)}, bf16[4,96,512]{2,1,0:T(8,128)(2,1)S(1)}, u32[]{:S(2)}, u32[]{:S(2)}) collective-permute-start(bf16[4,96,512]{2,1,0:T(8,128)(2,1)S(1)} %fusion.28), channel_id=1, source_target_pairs={{0,2},{1,3},{2,0},{3,1},{4,6},{5,7},{6,4},{7,5},{8,10},{9,11},{10,... | collective-permute-start | bytes 1179656 | tf_op jit(solution)/shard_map/ppermute | solution.py:23
  222.1 13.0 %slice-start = ((s8[5242880]{0:T(1024)(128)(4,1)}), s8[1048576]{0:T(1024)(128)(4,1)S(1)}, s32[]{:S(2)}) async-start(s8[5242880]{0:T(1024)(128)(4,1)} %bitcast.183), calls=%async_computation.3 | async-start | bytes 2097152
  222.5 10.2 %collective-permute-start.10 = (bf16[4,96,512]{2,1,0:T(8,128)(2,1)S(1)}, bf16[4,96,512]{2,1,0:T(8,128)(2,1)S(1)}, u32[]{:S(2)}, u32[]{:S(2)}) collective-permute-start(bf16[4,96,512]{2,1,0:T(8,128)(2,1)S(1)} %get-tuple-element.56), channel_id=1, source_target_pairs={{0,1},{1,0},{2,3},{3,2},{4,5},{5,4},{6,7},{7,6},{8,9},{9,8},{10,11... | collective-permute-start | bytes 1179656 | tf_op jit(solution)/shard_map/ppermute | solution.py:23
  224.1 11.0 %slice-start.1 = ((s8[5242880]{0:T(1024)(128)(4,1)}), s8[4194304]{0:T(1024)(128)(4,1)S(1)}, s32[]{:S(2)}) async-start(s8[5242880]{0:T(1024)(128)(4,1)} %bitcast.183), calls=%async_computation.4 | async-start | bytes 8388608
  224.2 10.3 %collective-permute-start.14 = (bf16[4,96,512]{2,1,0:T(8,128)(2,1)S(1)}, bf16[4,96,512]{2,1,0:T(8,128)(2,1)S(1)}, u32[]{:S(2)}, u32[]{:S(2)}) collective-permute-start(bf16[4,96,512]{2,1,0:T(8,128)(2,1)S(1)} %get-tuple-element.57), channel_id=1, source_target_pairs={{0,2},{1,3},{2,0},{3,1},{4,6},{5,7},{6,4},{7,5},{8,10},{9,11},{10,... | collective-permute-start | bytes 1179656 | tf_op jit(solution)/shard_map/ppermute | solution.py:23
  232.7 2.4 copy-start.10
  232.8 18.1 %collective-permute-start.11 = (bf16[4,2,96,512]{3,2,0,1:T(8,128)(2,1)S(1)}, bf16[4,2,96,512]{3,2,0,1:T(8,128)(2,1)S(1)}, u32[]{:S(2)}, u32[]{:S(2)}) collective-permute-start(bf16[4,2,96,512]{3,2,0,1:T(8,128)(2,1)S(1)} %pad_maximum_fusion.6), channel_id=1, source_target_pairs={{0,2},{1,3},{2,0},{3,1},{4,6},{5,7},{6,4},{7,5},{8,10},{9,11},{10,... | collective-permute-start | bytes 2359304 | tf_op jit(solution)/shard_map/ppermute | solution.py:23
  234.6 17.1 %collective-permute-start.15 = (bf16[4,2,96,512]{3,2,0,1:T(8,128)(2,1)S(1)}, bf16[4,2,96,512]{3,2,0,1:T(8,128)(2,1)S(1)}, u32[]{:S(2)}, u32[]{:S(2)}) collective-permute-start(bf16[4,2,96,512]{3,2,0,1:T(8,128)(2,1)S(1)} %pad_maximum_fusion.7), channel_id=1, source_target_pairs={{0,1},{1,0},{2,3},{3,2},{4,5},{5,4},{6,7},{7,6},{8,9},{9,8},{10,11... | collective-permute-start | bytes 2359304 | tf_op jit(solution)/shard_map/ppermute | solution.py:23
Sparse Core Ops, SparseCore 0:
  9.7 86.3 all-gather.2
  97.7 76.3 all-gather.4

commit v2 on v1

v2 whole, which is shorter than its diff:
```python
import functools
import math

import jax
import jax.numpy as jnp
from jax import lax
from jax.experimental import pallas as pl
from jax.experimental.pallas import tpu as pltpu
from jax.sharding import PartitionSpec as P

beta_first = 0.9
beta_second = 0.99
beta_public = 0.9
public_epsilon = 0.001
adam_epsilon = 1e-08
clip_factor = 0.6
noise_level = 4.0
learn_rate = 0.01
contract_rows = (((0,), (0,)), ((), ()))


MESH = pl.DeviceIdType.MESH
CORES = 2


def errors_kernel(
    pub_x, prv_x, pub_t, prv_t, w_ref,
    pub_all, prv_all, pub_d, prv_d,
    pub_aims, prv_aims, pub_send, prv_send, pub_recv, prv_recv, pub_own, prv_own, pub_y, prv_y,
    x_recv, up_sem, down_sem, core_sem, aim_recv, aim_sent, rs_recv, rs_sent, ag_recv, ag_sent,
):
    replicas = lax.axis_size("replica")
    tiles = lax.axis_size("tile")
    r = lax.axis_index("replica")
    t = lax.axis_index("tile")
    chips = replicas // CORES
    z = r // CORES
    c = r % CORES
    cols = w_ref.shape[1]
    inner = jnp.minimum(z, chips - 1 - z)
    phases = (
        (pub_x, pub_t, pub_all, pub_d, pub_aims, pub_send, pub_recv, pub_own, pub_y),
        (prv_x, prv_t, prv_all, prv_d, prv_aims, prv_send, prv_recv, prv_own, prv_y),
    )

    def to(src, dst, sent, got, replica, tile):
        return pltpu.make_async_remote_copy(
            src_ref=src, dst_ref=dst, send_sem=sent, recv_sem=got,
            device_id=(replica, tile), device_id_type=MESH,
        )

    def chip_at(i):
        k = (i + 1) // 2
        paired = jnp.where(i % 2 == 1, z - k, z + k)
        rest = jnp.where(z < chips - 1 - z, z + (i - inner), z - (i - inner))
        return jnp.where(i <= 2 * inner, paired, rest)

    def token_copy(f, q, sent, replica):
        ref = phases[f][2].at[q]
        return to(ref, ref, sent, x_recv.at[f, q], replica, t)

    def aim_copy(f, d):
        other = (r + d) % replicas
        ref = phases[f][1].at[:, pl.ds(pl.multiple_of(other * cols, cols), cols)]
        return to(ref, phases[f][4].at[d - 1], aim_sent.at[f, d - 1], aim_recv.at[f, d - 1], other, t)

    def part_copy(f, q, d):
        there = (t + d) % tiles
        return to(
            phases[f][5].at[q, there], phases[f][6].at[q, d - 1],
            rs_sent.at[f, q, d - 1], rs_recv.at[f, q, d - 1], r, there,
        )

    def error_copy(f, q, d):
        there = (t + d) % tiles
        ref = phases[f][3].at[q, t]
        return to(ref, ref, ag_sent.at[f, q, d - 1], ag_recv.at[f, q, d - 1], r, there)

    def error_arrival(f, q, d):
        ref = phases[f][3].at[q, (t + tiles - d) % tiles]
        return to(ref, ref, ag_sent.at[f, q, d - 1], ag_recv.at[f, q, d - 1], r, (t + tiles - d) % tiles)

    barrier = pltpu.get_barrier_semaphore()
    for d in range(1, replicas):
        pl.semaphore_signal(barrier, inc=1, device_id=((r + d) % replicas, t), device_id_type=MESH)
    for d in range(1, tiles):
        pl.semaphore_signal(barrier, inc=1, device_id=(r, (t + d) % tiles), device_id_type=MESH)
    pub_all[r] = pub_x[...]
    prv_all[r] = prv_x[...]
    pl.semaphore_wait(barrier, replicas + tiles - 2)

    def along(f, i, chip):
        mine = chip * CORES + c

        @pl.when(jnp.logical_and(chip <= z, z < chips - 1))
        def _():
            token_copy(f, mine, up_sem.at[f, i], r + CORES).start()

        @pl.when(jnp.logical_and(chip >= z, z > 0))
        def _():
            token_copy(f, mine, down_sem.at[f, i], r - CORES).start()

    def along_done(f, i):
        chip = chip_at(i)
        mine = chip * CORES + c

        @pl.when(jnp.logical_and(chip <= z, z < chips - 1))
        def _():
            token_copy(f, mine, up_sem.at[f, i], r + CORES).wait_send()

        @pl.when(jnp.logical_and(chip >= z, z > 0))
        def _():
            token_copy(f, mine, down_sem.at[f, i], r - CORES).wait_send()

    def partial(f, q):
        x_all, send, own, y = phases[f][2], phases[f][5], phases[f][7], phases[f][8]
        sub = y.shape[1]
        out = jnp.dot(x_all[q], w_ref[...], preferred_element_type=jnp.float32)
        for at in range(tiles):
            part = out[at * sub : (at + 1) * sub]
            y[at] = part
            send[q, at] = part.astype(jnp.bfloat16)
        for d in range(1, tiles):
            part_copy(f, q, d).start()
        own[q] = y[t]

    def finish(f, q):
        d_all, aims, recv, own = phases[f][3], phases[f][4], phases[f][6], phases[f][7]
        gap = (r + replicas - q) % replicas

        @pl.when(gap > 0)
        def _():
            to(aims.at[gap - 1], aims.at[gap - 1], aim_sent.at[f, gap - 1], aim_recv.at[f, gap - 1], q, t).wait_recv()
            own[q] = own[q] - aims[gap - 1].astype(jnp.float32)

        @pl.when(gap == 0)
        def _():
            mine = phases[f][1][:, pl.ds(pl.multiple_of(r * cols, cols), cols)]
            own[q] = own[q] - mine.astype(jnp.float32)

        total = own[q]
        for d in range(1, tiles):
            part_copy(f, q, d).wait_recv()
            total = total + recv[q, d - 1].astype(jnp.float32)
        d_all[q, t] = total.astype(jnp.bfloat16)
        for d in range(1, tiles):
            error_copy(f, q, d).start()

    def phase(f):
        def body(i, carry):
            @pl.when(i < chips)
            def _():
                chip = chip_at(i)
                mine = chip * CORES + c
                other = chip * CORES + 1 - c

                @pl.when(i > 0)
                def _():
                    token_copy(f, mine, up_sem.at[f, i], r).wait_recv()

                if f == 0:
                    along(f, i, chip)
                else:
                    @pl.when(i > 0)
                    def _():
                        along(f, i, chip)
                token_copy(f, mine, core_sem.at[f, i], z * CORES + 1 - c).start()

                @pl.when(i == 0)
                def _():
                    for d in range(1, replicas):
                        aim_copy(f, d).start()

                if f == 0:
                    @pl.when(i == min(1, chips - 1))
                    def _():
                        along(1, 0, z)

                partial(f, mine)
                token_copy(f, other, core_sem.at[f, i], r).wait_recv()
                partial(f, other)

            @pl.when(i > 0)
            def _():
                chip = chip_at(i - 1)
                finish(f, chip * CORES + c)
                finish(f, chip * CORES + 1 - c)

            return carry

        lax.fori_loop(0, chips + 1, body, 0)

    phase(0)
    phase(1)

    def close(f):
        def body(q, carry):
            for d in range(1, tiles):
                error_arrival(f, q, d).wait_recv()
                error_copy(f, q, d).wait_send()
                part_copy(f, q, d).wait_send()
            return carry

        lax.fori_loop(0, replicas, body, 0)

        def sent(i, carry):
            along_done(f, i)
            token_copy(f, chip_at(i) * CORES + c, core_sem.at[f, i], r).wait_send()
            return carry

        lax.fori_loop(0, chips, sent, 0)
        for d in range(1, replicas):
            aim_copy(f, d).wait_send()

    close(0)
    close(1)


def gathered_errors(pub_x, prv_x, pub_t, prv_t, w_half):
    replicas = lax.axis_size("replica")
    tiles = lax.axis_size("tile")
    chips = replicas // CORES
    rows, cols = w_half.shape
    half, full = jnp.bfloat16, jnp.float32
    spans = (pub_x.shape[0], prv_x.shape[0])
    subs = [span // tiles for span in spans]
    vmem = pl.BlockSpec(memory_space=pltpu.VMEM)
    scratch = [pltpu.VMEM((replicas - 1, sub, cols), half) for sub in subs]
    scratch += [pltpu.VMEM((replicas, tiles, sub, cols), half) for sub in subs]
    scratch += [pltpu.VMEM((replicas, tiles - 1, sub, cols), half) for sub in subs]
    scratch += [pltpu.VMEM((replicas, sub, cols), full) for sub in subs]
    scratch += [pltpu.VMEM((tiles, sub, cols), full) for sub in subs]
    sems = [(2, replicas), (2, chips), (2, chips), (2, chips), (2, replicas - 1), (2, replicas - 1)]
    sems += [(2, replicas, tiles - 1)] * 4
    scratch += [pltpu.SemaphoreType.DMA(shape) for shape in sems]
    flops = 2 * replicas * sum(spans) * rows * cols
    return pl.pallas_call(
        errors_kernel,
        out_shape=[jax.ShapeDtypeStruct((replicas, span, rows), half) for span in spans]
        + [jax.ShapeDtypeStruct((replicas, tiles, sub, cols), half) for sub in subs],
        in_specs=[vmem] * 5,
        out_specs=[vmem] * 4,
        scratch_shapes=scratch,
        compiler_params=pltpu.CompilerParams(
            collective_id=0, has_side_effects=True, vmem_limit_bytes=56 * 1024 * 1024
        ),
        cost_estimate=pl.CostEstimate(flops=flops, bytes_accessed=2 * replicas * sum(spans) * rows, transcendentals=0),
        name="gathered_errors",
    )(pub_x, prv_x, pub_t, prv_t, w_half)


def norm_kernel(x_ref, d_ref, p_ref, out_ref):
    total = jnp.zeros(out_ref.shape[1:], jnp.float32)
    rows = x_ref.shape[1]
    step = 256 if rows % 256 == 0 else 64
    for at in range(0, rows, step):
        grads = lax.dot_general(
            x_ref[:, at : at + step], d_ref[...], contract_rows, preferred_element_type=jnp.float32
        )
        scaled = grads * p_ref[at : at + step, :]
        total += jnp.sum((scaled * scaled).reshape(step // 8, 8, -1), axis=0)
    out_ref[0] = total


def example_squares(tokens, delta, precond, examples):
    slots, rows = tokens.shape
    seq_len = slots // examples
    cols = delta.shape[1]
    parts = pl.pallas_call(
        norm_kernel,
        grid=(examples,),
        in_specs=[
            pl.BlockSpec((seq_len, rows), lambda j: (j, 0)),
            pl.BlockSpec((seq_len, cols), lambda j: (j, 0)),
            pl.BlockSpec((rows, cols), lambda j: (0, 0)),
        ],
        out_specs=pl.BlockSpec((1, 8, cols), lambda j: (j, 0, 0)),
        out_shape=jax.ShapeDtypeStruct((examples, 8, cols), jnp.float32),
        compiler_params=pltpu.CompilerParams(vmem_limit_bytes=40 * 1024 * 1024),
        cost_estimate=pl.CostEstimate(
            flops=2 * slots * rows * cols, bytes_accessed=2 * slots * (rows + cols), transcendentals=0
        ),
        name="example_norms",
    )(tokens, delta, precond)
    return jnp.sum(parts, axis=(1, 2))


def update_kernel(
    total_examples, noise_scale, f_ref, x_ref, d_ref, p_ref, n_ref, m_ref, v_ref, w_ref,
    new_w, new_m, new_v, weighted,
):
    examples = f_ref.shape[0]
    seq_len = d_ref.shape[0] // examples

    @pl.when(pl.program_id(0) == 0)
    def _():
        for j in range(examples):
            at = slice(j * seq_len, (j + 1) * seq_len)
            weighted[at, :] = (f_ref[j] * d_ref[at, :].astype(jnp.float32)).astype(jnp.bfloat16)

    summed = p_ref[...] * lax.dot_general(
        x_ref[...], weighted[...], contract_rows, preferred_element_type=jnp.float32
    )
    gradient = (summed + noise_scale * n_ref[...]) * (1.0 / total_examples)
    first = beta_first * m_ref[...] + (1.0 - beta_first) * gradient
    second = beta_second * v_ref[...] + (1.0 - beta_second) * gradient * gradient
    new_m[...] = first
    new_v[...] = second
    first_hat = first * (1.0 / (1.0 - beta_first**2))
    second_hat = second * (1.0 / (1.0 - beta_second**2))
    new_w[...] = w_ref[...] - learn_rate * first_hat / (jnp.sqrt(second_hat) + adam_epsilon)


def update(factors, tokens, delta, precond, noise, first, second, weight, noise_scale):
    slots, rows = tokens.shape
    cols = delta.shape[1]
    examples = factors.shape[0]
    step = 256 if rows % 256 == 0 else rows
    state = pl.BlockSpec((step, cols), lambda i: (i, 0))
    return pl.pallas_call(
        functools.partial(update_kernel, examples, noise_scale),
        grid=(rows // step,),
        in_specs=[
            pl.BlockSpec(memory_space=pltpu.SMEM),
            pl.BlockSpec((slots, step), lambda i: (0, i)),
            pl.BlockSpec((slots, cols), lambda i: (0, 0)),
        ]
        + [state] * 5,
        out_specs=[state] * 3,
        out_shape=[jax.ShapeDtypeStruct((rows, cols), jnp.float32)] * 3,
        scratch_shapes=[pltpu.VMEM((slots, cols), jnp.bfloat16)],
        compiler_params=pltpu.CompilerParams(vmem_limit_bytes=48 * 1024 * 1024),
        cost_estimate=pl.CostEstimate(
            flops=2 * slots * rows * cols,
            bytes_accessed=2 * slots * (rows + cols) + 32 * rows * cols,
            transcendentals=rows * cols,
        ),
        name="update",
    )(factors, tokens, delta, precond, noise, first, second, weight)


def on_device(
    public_tokens,
    public_targets,
    private_tokens,
    private_targets,
    token_counts,
    weight,
    public_moment,
    adam_first,
    adam_second,
    noise_draw,
):
    replicas = lax.axis_size("replica")
    tiles = lax.axis_size("tile")
    examples_here = token_counts.shape[1]
    examples_total = examples_here * replicas
    slots_here = private_tokens.shape[0]
    seq_len = slots_here // examples_here
    width = weight.shape[0] * tiles
    columns = weight.shape[1] * replicas
    cols = weight.shape[1]
    public_total = public_tokens.shape[0] * replicas

    limits = jnp.repeat(token_counts[0], seq_len, total_repeat_length=slots_here)
    live = jnp.arange(slots_here, dtype=jnp.int32) % seq_len < limits
    private_tokens = jnp.where(live[:, None], private_tokens, jnp.zeros((), private_tokens.dtype))

    w_half = weight.astype(jnp.bfloat16)
    public_all, private_all, public_delta, private_delta = gathered_errors(
        public_tokens, private_tokens, public_targets, private_targets, w_half
    )
    public_all = public_all.reshape(public_total, -1)
    public_delta = public_delta.reshape(public_total, cols)
    private_all = private_all.reshape(slots_here * replicas, -1)
    private_delta = private_delta.reshape(slots_here * replicas, cols)

    public_grad = lax.dot_general(
        public_all, public_delta, contract_rows, preferred_element_type=jnp.float32
    ) / math.sqrt(public_total)
    new_public = beta_public * public_moment + (1.0 - beta_public) * public_grad * public_grad
    precond = 1.0 / (jnp.sqrt(new_public) + public_epsilon)

    squares = example_squares(private_all, private_delta, precond, examples_total)
    squares = lax.psum(squares, ("replica", "tile"))
    clip_norm = clip_factor * math.sqrt(seq_len * width * columns)
    factors = clip_norm / jnp.maximum(jnp.sqrt(squares), clip_norm)
    noise_scale = noise_level * clip_factor * math.sqrt(seq_len)
    new_weight, new_first, new_second = update(
        factors, private_all, private_delta, precond, noise_draw, adam_first, adam_second, weight, noise_scale
    )
    return (new_weight, new_first, new_second, new_public)


def solution(mesh):
    placed = (
        P("replica", "tile"),
        P(("replica", "tile"), None),
        P("replica", "tile"),
        P(("replica", "tile"), None),
        P("replica", None),
        P("tile", "replica"),
        P("tile", "replica"),
        P("tile", "replica"),
        P("tile", "replica"),
        P("tile", "replica"),
    )
    return jax.shard_map(
        on_device,
        mesh=mesh,
        in_specs=placed,
        out_specs=(
            P("tile", "replica"),
            P("tile", "replica"),
            P("tile", "replica"),
            P("tile", "replica"),
        ),
        check_vma=False,
    )
```

time: 344 us -> 272 us (0.79)
  Pallas kernels: 12.8 us -> 211 us
  waiting for transfers between devices: 181 us -> 0 us
  matrix products: 33.4 us -> 8.6 us
  starting transfers between devices: 23.7 us -> 0 us
  other arithmetic: 30.7 us -> 7.5 us
  between operations: 14.4 us -> 0.7 us
    pallas_call x0 -> x2, Pallas kernels: none -> 198 us  [the longest x1 184 us: gathered_errors(): pl.pallas_call(errors_kernel, out_shape=[jax.ShapeDtypeStruct((replicas,...]
    all_gather x2 -> x0, waiting for transfers between devices: 109 us -> none  [the longest x1 72.8 us: on_device(): public_all = lax.all_gather(public_tokens, 'replica', axis=0, tiled=True)]
    ppermute x16 -> x0, waiting for transfers between devices: 72.3 us -> none  [swap(): return lax.ppermute(value, 'tile', [(i, i ^ bit) for i in range(size)])]
    dot_general x5 -> x0, matrix products: 27.9 us -> none  [the longest x1 15.9 us: on_device(): lax.dot_general(private_all, weighted, contract_rows, preferred_element_t...]
    ppermute x16 -> x0, starting transfers between devices: 17.3 us -> none  [swap(): return lax.ppermute(value, 'tile', [(i, i ^ bit) for i in range(size)])]
    select_n x1 -> x0, other arithmetic: 10.8 us -> none  [on_device(): jnp.repeat(factors, seq_len, total_repeat_length=slots_here * replicas)]
    all_to_all x1 -> x0, starting transfers between devices: 6.33 us -> none  [on_device(): lax.all_to_all(aims, 'replica', split_axis=1, concat_axis=0, tiled=True)]
    gather x2 -> x0, other arithmetic: 5.05 us -> none  [on_device(): jnp.repeat(factors, seq_len, total_repeat_length=slots_here * replicas)]
  transfers between devices with their start and end apart: 19 -> 0, of which waited for: 15 -> 0; matrix products, arithmetic and copies ran while one was open for 11% -> 0% of each run, Pallas kernels for 0% -> 0%
where the time goes in v2:
time: 272 us; the launch traced here: 271 us
  Pallas kernels  211 us (78%)
  blocking collectives  37 us (14%)
  matrix products  8.6 us (3%)
  other arithmetic  7.5 us (3%)
  local copies, waits for them, and re-layouts  6.34 us (2%)
    pallas_call x1, Pallas kernels, gathered_errors(): pl.pallas_call(errors_kernel, out_shape=[jax.ShapeDtypeStruct((replicas,...  184 us
    psum x1, blocking collectives, on_device(): squares = lax.psum(squares, ('replica', 'tile'))  37 us
    pallas_call x1, Pallas kernels, update(): pl.pallas_call(functools.partial(update_kernel, examples, noise_scale), g...  14.1 us
    pallas_call x1, Pallas kernels, example_squares(): pl.pallas_call(norm_kernel, grid=(examples,), in_specs=[pl.BlockSpec((seq...  12.8 us
    dot_general x1, matrix products, on_device(): lax.dot_general(public_all, public_delta, contract_rows, preferred_elemen...  8.6 us

profile of v2, /device:TPU:0, one launch (start us, length us, event | category | flops | bytes accessed | tf_op | source)
XLA Modules:
  0.0 270.8 jit_solution(9159721495640712872)
XLA Ops:
  0.6 1.4 fusion.9
  2.0 2.0 fusion.8
  4.0 2.3 broadcast_select_fusion.prv_x
  6.3 3.0 %convert_element_type.3.w_ref = bf16[1280,512]{1,0:T(8,128)(2,1)} convert(f32[1280,512]{1,0:T(8,128)} %w_ref.1) | non-fusion elementwise | flops 655360 | bytes 3932160 | tf_op jit(solution)/shard_map/convert_element_type | solution.py:369
  9.2 0.0 copy-start.5
  9.2 183.8 %gathered_errors.1 = (bf16[8,256,1280]{2,1,0:T(8,128)(2,1)}, bf16[8,384,1280]{2,1,0:T(8,128)(2,1)}, bf16[8,4,64,512]{3,2,1,0:T(8,128)(2,1)}, bf16[8,4,96,512]{3,2,1,0:T(8,128)(2,1)}) custom-call(bf16[256,1280]{1,0:T(8,128)(2,1)} %pub_x.1, bf16[384,1280]{1,0:T(8,128)(2,1)} %broadcast_select_fusion.prv_x, bf16[64,4096]{1,0:T(8,128)(2,1)} %pub_t.1, ...), custom_call_target="tpu_custom_call" | custom-call | flops 6710886400 | bytes 13107200 | tf_op jit(solution)/shard_map/gathered_errors/pallas_call | solution.py:237
  193.0 0.0 copy-done.5
  193.0 0.0 copy-start
  193.1 0.0 copy-start.1
  193.1 8.6 %add_divide_fusion = (f32[1280,512]{1,0:T(8,128)S(1)}, f32[1280,512]{1,0:T(8,128)}) fusion(f32[1280,512]{1,0:T(8,128)S(1)} %copy-done.5, bf16[2048,1280]{1,0:T(8,128)(2,1)} %bitcast.33, bf16[2048,512]{1,0:T(8,128)(2,1)} %bitcast.34), kind=kOutput, calls=%fused_computation | convolution fusion | flops 2688942080 | bytes 15204352 | tf_op jit(solution)/shard_map/dot_general | solution.py:378
  201.7 0.0 copy-done
  201.7 0.0 copy-done.1
  201.7 12.8 %example_norms.1 = f32[24,8,512]{2,1,0:T(8,128)S(1)} custom-call(bf16[3072,1280]{1,0:T(8,128)(2,1)S(1)} %bitcast.30, bf16[3072,512]{1,0:T(8,128)(2,1)S(1)} %bitcast.32, f32[1280,512]{1,0:T(8,128)S(1)} %get-tuple-element.30.p_ref), custom_call_target="tpu_custom_call" | custom-call | flops 4026531840 | bytes 11010048 | tf_op jit(solution)/shard_map/example_norms/pallas_call | solution.py:269
  214.5 0.0 copy-start.3
  214.5 1.5 copy-done.3
  215.9 0.3 reduce_sum.9
  216.2 37.0 %psum.7 = f32[24]{0:T(128)S(1)} all-reduce(f32[24]{0:T(128)S(1)} %reduce_sum.9), channel_id=1, replica_groups=mesh['replica'=8,'tile'=4] {'replica','tile'}, use_global_device_ids=true, to_apply=%region_1.2 | all-reduce | flops 24 | bytes 192 | tf_op jit(solution)/shard_map/psum | solution.py:385
  253.2 0.0 copy-start.2
  253.2 1.7 copy-done.2
  255.0 0.0 copy-start.4
  255.0 1.7 copy-done.4
  256.7 14.1 %update.1 = (f32[1280,512]{1,0:T(8,128)}, f32[1280,512]{1,0:T(8,128)}, f32[1280,512]{1,0:T(8,128)}) custom-call(f32[24]{0:T(128)S(1)} %maximum_divide_fusion.f_ref, bf16[3072,1280]{1,0:T(8,128)(2,1)} %bitcast.29, bf16[3072,512]{1,0:T(8,128)(2,1)} %bitcast.31, f32[1280,512]{1,0:T(8,128)S(1)} %copy-done.4, f32[1280,512]{1,0:T(8,128)S(1)} %copy-done.2, ...), custom_call_target="tpu_custom_call" | custom-call | flops 4026531840 | bytes 31981568 | tf_op jit(solution)/shard_map/update/pallas_call | solution.py:320
  (3 shorter events, 0.0 us)
Async XLA Ops:
  9.2 183.8 %copy-start.5 = (f32[1280,512]{1,0:T(8,128)S(1)}, f32[1280,512]{1,0:T(8,128)}, u32[]{:S(2)}) copy-start(f32[1280,512]{1,0:T(8,128)} %param.18) | copy-start | bytes 7864324
  193.0 8.6 %copy-start = (bf16[8,384,1280]{2,1,0:T(8,128)(2,1)S(1)}, bf16[8,384,1280]{2,1,0:T(8,128)(2,1)}, u32[]{:S(2)}) copy-start(bf16[8,384,1280]{2,1,0:T(8,128)(2,1)} %get-tuple-element.23) | copy-start | bytes 23592964
  193.1 8.6 %copy-start.1 = (bf16[8,4,96,512]{3,2,1,0:T(8,128)(2,1)S(1)}, bf16[8,4,96,512]{3,2,1,0:T(8,128)(2,1)}, u32[]{:S(2)}) copy-start(bf16[8,4,96,512]{3,2,1,0:T(8,128)(2,1)} %get-tuple-element.24) | copy-start | bytes 9437188
  214.5 1.5 copy-start.3
  253.2 1.8 copy-start.2
  255.0 1.7 copy-start.4

commit v3 on v2

--- a/solution.py
+++ b/solution.py
@@ -24,10 +24,13 @@
 
 
 def errors_kernel(
-    pub_x, prv_x, pub_t, prv_t, w_ref,
-    pub_all, prv_all, pub_d, prv_d,
+    root, clip_norm,
+    pub_x, prv_x, pub_t, prv_t, counts, weight, moment,
+    prv_all, prv_d, new_public, precond, factors,
+    pub_all, pub_d, w_ref, squares, tile_squares, all_squares,
     pub_aims, prv_aims, pub_send, prv_send, pub_recv, prv_recv, pub_own, prv_own, pub_y, prv_y,
     x_recv, up_sem, down_sem, core_sem, aim_recv, aim_sent, rs_recv, rs_sent, ag_recv, ag_sent,
+    tile_recv, tile_sent, all_recv, all_sent,
 ):
     replicas = lax.axis_size("replica")
     tiles = lax.axis_size("tile")
@@ -51,8 +54,9 @@
 
     def chip_at(i):
         k = (i + 1) // 2
-        paired = jnp.where(i % 2 == 1, z - k, z + k)
-        rest = jnp.where(z < chips - 1 - z, z + (i - inner), z - (i - inner))
+        longer = jnp.where(z < chips - 1 - z, 1, -1)
+        paired = jnp.where(i % 2 == 1, z + longer * k, z - longer * k)
+        rest = z + longer * (i - inner)
         return jnp.where(i <= 2 * inner, paired, rest)
 
     def token_copy(f, q, sent, replica):
@@ -86,7 +90,14 @@
     for d in range(1, tiles):
         pl.semaphore_signal(barrier, inc=1, device_id=(r, (t + d) % tiles), device_id_type=MESH)
     pub_all[r] = pub_x[...]
-    prv_all[r] = prv_x[...]
+    examples = counts.shape[1]
+    seq_len = prv_x.shape[0] // examples
+    row = lax.broadcasted_iota(jnp.int32, (seq_len, 1), 0)
+    for e in range(examples):
+        live = (row < counts[0, e]).astype(jnp.float32)
+        at = slice(e * seq_len, (e + 1) * seq_len)
+        prv_all[r, at, :] = (prv_x[at, :].astype(jnp.float32) * live).astype(jnp.bfloat16)
+    w_ref[...] = weight[...].astype(jnp.bfloat16)
     pl.semaphore_wait(barrier, replicas + tiles - 2)
 
     def along(f, i, chip):
@@ -146,6 +157,64 @@
         for d in range(1, tiles):
             error_copy(f, q, d).start()
 
+    def arrived(f, q):
+        for d in range(1, tiles):
+            error_arrival(f, q, d).wait_recv()
+
+    rows = weight.shape[0]
+    step = 256 if rows % 256 == 0 else rows
+
+    def public_update():
+        def waiting(q, carry):
+            arrived(0, q)
+            return carry
+
+        lax.fori_loop(0, replicas, waiting, 0)
+        total = replicas * pub_x.shape[0]
+        errors = pub_d[...].reshape(total, cols)
+        for at in range(0, rows, step):
+            tokens = pub_all[:, :, at : at + step].reshape(total, step)
+            grads = lax.dot_general(tokens, errors, contract_rows, preferred_element_type=jnp.float32)
+            grads = grads * (1.0 / root)
+            moved = beta_public * moment[at : at + step, :] + (1.0 - beta_public) * grads * grads
+            new_public[at : at + step, :] = moved
+            precond[at : at + step, :] = 1.0 / (jnp.sqrt(moved) + public_epsilon)
+
+    def norms(chip):
+        def body(which, carry):
+            q = chip * CORES + (c + which) % CORES
+            arrived(1, q)
+            parts = [prv_d[q, at] for at in range(tiles)]
+            if parts[0].shape[0] % 16 == 0:
+                errors = jnp.concatenate(parts, axis=0)
+            else:
+                errors = jnp.concatenate([part.astype(jnp.float32) for part in parts], axis=0)
+                errors = errors.astype(jnp.bfloat16)
+            for e in range(examples):
+                span = slice(e * seq_len, (e + 1) * seq_len)
+                total = jnp.zeros((8, cols), jnp.float32)
+                for at in range(0, rows, step):
+                    grads = lax.dot_general(
+                        prv_all[q, span, at : at + step], errors[span],
+                        contract_rows, preferred_element_type=jnp.float32,
+                    )
+                    scaled = grads * precond[at : at + step, :]
+                    total += jnp.sum((scaled * scaled).reshape(step // 8, 8, cols), axis=0)
+                line = jnp.sum(total, axis=0, keepdims=True)
+                line = sum(line[:, at : at + 128] for at in range(0, cols, 128))
+                squares[pl.ds(q * examples + e, 1), :] = line
+            return carry
+
+        lax.fori_loop(0, CORES, body, 0)
+
+    def tile_copy(d):
+        return to(squares, tile_squares.at[d - 1], tile_sent.at[d - 1], tile_recv.at[d - 1], r, (t + d) % tiles)
+
+    def all_copy(d):
+        return to(
+            factors, all_squares.at[d - 1], all_sent.at[d - 1], all_recv.at[d - 1], (r + d) % replicas, t
+        )
+
     def phase(f):
         def body(i, carry):
             @pl.when(i < chips)
@@ -180,23 +249,51 @@
                 token_copy(f, other, core_sem.at[f, i], r).wait_recv()
                 partial(f, other)
 
-            @pl.when(i > 0)
+            @pl.when(jnp.logical_and(i > 0, i <= chips))
             def _():
                 chip = chip_at(i - 1)
                 finish(f, chip * CORES + c)
                 finish(f, chip * CORES + 1 - c)
 
+            if f == 1:
+                @pl.when(i == 1)
+                def _():
+                    public_update()
+
+                @pl.when(i > 1)
+                def _():
+                    norms(chip_at(i - 2))
+
             return carry
 
-        lax.fori_loop(0, chips + 1, body, 0)
+        lax.fori_loop(0, chips + 1 + f, body, 0)
 
     phase(0)
     phase(1)
+
+    for d in range(1, tiles):
+        tile_copy(d).start()
+    for d in range(1, tiles):
+        tile_copy(d).wait_recv()
+    total = squares[...]
+    for d in range(1, tiles):
+        total = total + tile_squares[d - 1]
+    factors[...] = total
+    for d in range(1, replicas):
+        all_copy(d).start()
+    for d in range(1, replicas):
+        all_copy(d).wait()
+    for d in range(1, replicas):
+        total = total + all_squares[d - 1]
+    total = jnp.sum(total, axis=1, keepdims=True)
+    factor = clip_norm / jnp.maximum(jnp.sqrt(total), clip_norm)
+    factors[...] = jnp.broadcast_to(factor, factors.shape)
+    for d in range(1, tiles):
+        tile_copy(d).wait_send()
 
     def close(f):
         def body(q, carry):
             for d in range(1, tiles):
-                error_arrival(f, q, d).wait_recv()
                 error_copy(f, q, d).wait_send()
                 part_copy(f, q, d).wait_send()
             return carry
@@ -216,73 +313,49 @@
     close(1)
 
 
-def gathered_errors(pub_x, prv_x, pub_t, prv_t, w_half):
+def gathered_errors(pub_x, prv_x, pub_t, prv_t, counts, weight, moment, root, clip_norm):
     replicas = lax.axis_size("replica")
     tiles = lax.axis_size("tile")
     chips = replicas // CORES
-    rows, cols = w_half.shape
+    rows, cols = weight.shape
     half, full = jnp.bfloat16, jnp.float32
     spans = (pub_x.shape[0], prv_x.shape[0])
     subs = [span // tiles for span in spans]
+    examples = counts.shape[1] * replicas
     vmem = pl.BlockSpec(memory_space=pltpu.VMEM)
-    scratch = [pltpu.VMEM((replicas - 1, sub, cols), half) for sub in subs]
+    tokens = [(replicas, span, rows) for span in spans]
+    errors = [(replicas, tiles, sub, cols) for sub in subs]
+    scratch = [pltpu.VMEM(tokens[0], half), pltpu.VMEM(errors[0], half), pltpu.VMEM((rows, cols), half)]
+    scratch += [pltpu.VMEM(shape + (examples, 128), full) for shape in ((), (tiles - 1,), (replicas - 1,))]
+    scratch += [pltpu.VMEM((replicas - 1, sub, cols), half) for sub in subs]
     scratch += [pltpu.VMEM((replicas, tiles, sub, cols), half) for sub in subs]
     scratch += [pltpu.VMEM((replicas, tiles - 1, sub, cols), half) for sub in subs]
     scratch += [pltpu.VMEM((replicas, sub, cols), full) for sub in subs]
     scratch += [pltpu.VMEM((tiles, sub, cols), full) for sub in subs]
     sems = [(2, replicas), (2, chips), (2, chips), (2, chips), (2, replicas - 1), (2, replicas - 1)]
     sems += [(2, replicas, tiles - 1)] * 4
+    sems += [(tiles - 1,)] * 2 + [(replicas - 1,)] * 2
     scratch += [pltpu.SemaphoreType.DMA(shape) for shape in sems]
-    flops = 2 * replicas * sum(spans) * rows * cols
+    flops = 4 * replicas * sum(spans) * rows * cols
+    state = jax.ShapeDtypeStruct((rows, cols), full)
     return pl.pallas_call(
-        errors_kernel,
-        out_shape=[jax.ShapeDtypeStruct((replicas, span, rows), half) for span in spans]
-        + [jax.ShapeDtypeStruct((replicas, tiles, sub, cols), half) for sub in subs],
-        in_specs=[vmem] * 5,
-        out_specs=[vmem] * 4,
+        functools.partial(errors_kernel, root, clip_norm),
+        out_shape=[
+            jax.ShapeDtypeStruct(tokens[1], half),
+            jax.ShapeDtypeStruct(errors[1], half),
+            state,
+            state,
+            jax.ShapeDtypeStruct((examples, 128), full),
+        ],
+        in_specs=[vmem] * 4 + [pl.BlockSpec(memory_space=pltpu.SMEM)] + [vmem] * 2,
+        out_specs=[vmem] * 5,
         scratch_shapes=scratch,
         compiler_params=pltpu.CompilerParams(
-            collective_id=0, has_side_effects=True, vmem_limit_bytes=56 * 1024 * 1024
+            collective_id=0, has_side_effects=True, vmem_limit_bytes=58 * 1024 * 1024
         ),
         cost_estimate=pl.CostEstimate(flops=flops, bytes_accessed=2 * replicas * sum(spans) * rows, transcendentals=0),
         name="gathered_errors",
-    )(pub_x, prv_x, pub_t, prv_t, w_half)
-
-
-def norm_kernel(x_ref, d_ref, p_ref, out_ref):
-    total = jnp.zeros(out_ref.shape[1:], jnp.float32)
-    rows = x_ref.shape[1]
-    step = 256 if rows % 256 == 0 else 64
-    for at in range(0, rows, step):
-        grads = lax.dot_general(
-            x_ref[:, at : at + step], d_ref[...], contract_rows, preferred_element_type=jnp.float32
-        )
-        scaled = grads * p_ref[at : at + step, :]
-        total += jnp.sum((scaled * scaled).reshape(step // 8, 8, -1), axis=0)
-    out_ref[0] = total
-
-
-def example_squares(tokens, delta, precond, examples):
-    slots, rows = tokens.shape
-    seq_len = slots // examples
-    cols = delta.shape[1]
-    parts = pl.pallas_call(
-        norm_kernel,
-        grid=(examples,),
-        in_specs=[
-            pl.BlockSpec((seq_len, rows), lambda j: (j, 0)),
-            pl.BlockSpec((seq_len, cols), lambda j: (j, 0)),
-            pl.BlockSpec((rows, cols), lambda j: (0, 0)),
-        ],
-        out_specs=pl.BlockSpec((1, 8, cols), lambda j: (j, 0, 0)),
-        out_shape=jax.ShapeDtypeStruct((examples, 8, cols), jnp.float32),
-        compiler_params=pltpu.CompilerParams(vmem_limit_bytes=40 * 1024 * 1024),
-        cost_estimate=pl.CostEstimate(
-            flops=2 * slots * rows * cols, bytes_accessed=2 * slots * (rows + cols), transcendentals=0
-        ),
-        name="example_norms",
-    )(tokens, delta, precond)
-    return jnp.sum(parts, axis=(1, 2))
+    )(pub_x, prv_x, pub_t, prv_t, counts, weight, moment)
 
 
 def update_kernel(
@@ -296,7 +369,7 @@
     def _():
         for j in range(examples):
             at = slice(j * seq_len, (j + 1) * seq_len)
-            weighted[at, :] = (f_ref[j] * d_ref[at, :].astype(jnp.float32)).astype(jnp.bfloat16)
+            weighted[at, :] = (f_ref[j : j + 1, :1] * d_ref[at, :].astype(jnp.float32)).astype(jnp.bfloat16)
 
     summed = p_ref[...] * lax.dot_general(
         x_ref[...], weighted[...], contract_rows, preferred_element_type=jnp.float32
@@ -321,7 +394,7 @@
         functools.partial(update_kernel, examples, noise_scale),
         grid=(rows // step,),
         in_specs=[
-            pl.BlockSpec(memory_space=pltpu.SMEM),
+            pl.BlockSpec((examples, 128), lambda i: (0, 0)),
             pl.BlockSpec((slots, step), lambda i: (0, i)),
             pl.BlockSpec((slots, cols), lambda i: (0, 0)),
         ]
@@ -354,7 +427,6 @@
     replicas = lax.axis_size("replica")
     tiles = lax.axis_size("tile")
     examples_here = token_counts.shape[1]
-    examples_total = examples_here * replicas
     slots_here = private_tokens.shape[0]
     seq_len = slots_here // examples_here
     width = weight.shape[0] * tiles
@@ -362,29 +434,13 @@
     cols = weight.shape[1]
     public_total = public_tokens.shape[0] * replicas
 
-    limits = jnp.repeat(token_counts[0], seq_len, total_repeat_length=slots_here)
-    live = jnp.arange(slots_here, dtype=jnp.int32) % seq_len < limits
-    private_tokens = jnp.where(live[:, None], private_tokens, jnp.zeros((), private_tokens.dtype))
-
-    w_half = weight.astype(jnp.bfloat16)
-    public_all, private_all, public_delta, private_delta = gathered_errors(
-        public_tokens, private_tokens, public_targets, private_targets, w_half
-    )
-    public_all = public_all.reshape(public_total, -1)
-    public_delta = public_delta.reshape(public_total, cols)
+    clip_norm = clip_factor * math.sqrt(seq_len * width * columns)
+    private_all, private_delta, new_public, precond, factors = gathered_errors(
+        public_tokens, private_tokens, public_targets, private_targets, token_counts, weight, public_moment,
+        math.sqrt(public_total), clip_norm,
+    )
     private_all = private_all.reshape(slots_here * replicas, -1)
     private_delta = private_delta.reshape(slots_here * replicas, cols)
-
-    public_grad = lax.dot_general(
-        public_all, public_delta, contract_rows, preferred_element_type=jnp.float32
-    ) / math.sqrt(public_total)
-    new_public = beta_public * public_moment + (1.0 - beta_public) * public_grad * public_grad
-    precond = 1.0 / (jnp.sqrt(new_public) + public_epsilon)
-
-    squares = example_squares(private_all, private_delta, precond, examples_total)
-    squares = lax.psum(squares, ("replica", "tile"))
-    clip_norm = clip_factor * math.sqrt(seq_len * width * columns)
-    factors = clip_norm / jnp.maximum(jnp.sqrt(squares), clip_norm)
     noise_scale = noise_level * clip_factor * math.sqrt(seq_len)
     new_weight, new_first, new_second = update(
         factors, private_all, private_delta, precond, noise_draw, adam_first, adam_second, weight, noise_scale

time: 272 us -> 219 us (0.81)
  blocking collectives: 37 us -> 0 us
  matrix products: 8.6 us -> 0 us
  other arithmetic: 7.5 us -> 0 us
  Pallas kernels: 211 us -> 214 us
    psum x1 -> x0, blocking collectives: 37 us -> none  [on_device(): squares = lax.psum(squares, ('replica', 'tile'))]
    dot_general x1 -> x0, matrix products: 8.6 us -> none  [on_device(): lax.dot_general(public_all, public_delta, contract_rows, preferred_elemen...]
    pallas_call x2 -> x1, Pallas kernels: 197 us -> 200 us  [gathered_errors(): pl.pallas_call(functools.partial(errors_kernel, root, clip_norm), out_sha...]
    convert_element_type x1 -> x0, other arithmetic: 2.96 us -> none  [on_device(): w_half = weight.astype(jnp.bfloat16)]
where the time goes in v3:
time: 219 us
  Pallas kernels  214 us (98%)
  local copies, waits for them, and re-layouts  3.94 us (2%)
    pallas_call x1, Pallas kernels, gathered_errors(): pl.pallas_call(functools.partial(errors_kernel, root, clip_norm), out_sha...  200 us
    pallas_call x1, Pallas kernels, update(): pl.pallas_call(functools.partial(update_kernel, examples, noise_scale), g...  14.6 us

profile of v3, /device:TPU:0, one launch (start us, length us, event | category | flops | bytes accessed | tf_op | source)
XLA Modules:
  0.0 218.9 jit_solution(1459866270503086313)
XLA Ops:
  0.6 0.0 copy-start
  0.6 199.7 %gathered_errors.1 = (bf16[8,384,1280]{2,1,0:T(8,128)(2,1)}, bf16[8,4,96,512]{3,2,1,0:T(8,128)(2,1)}, f32[1280,512]{1,0:T(8,128)}, f32[1280,512]{1,0:T(8,128)}, f32[24,128]{1,0:T(8,128)}) custom-call(bf16[256,1280]{1,0:T(8,128)(2,1)} %pub_x.1, bf16[384,1280]{1,0:T(8,128)(2,1)} %prv_x.1, bf16[64,4096]{1,0:T(8,128)(2,1)} %pub_t.1, bf16[96,4096]{1,0:T(8,128)(2,1)} %prv_t.1, ...), custom_call_target="tpu_custom_call" | custom-call | flops 13421772800 | bytes 13107200 | tf_op jit(solution)/shard_map/gathered_errors/pallas_call | solution.py:341
  200.3 0.0 copy-done
  200.4 0.0 copy-start.1
  200.4 1.7 copy-done.1
  202.1 0.0 copy-start.2
  202.1 0.7 copy-done.2
  202.8 0.0 copy-start.3
  202.8 14.6 %update.1 = (f32[1280,512]{1,0:T(8,128)}, f32[1280,512]{1,0:T(8,128)}, f32[1280,512]{1,0:T(8,128)}) custom-call(f32[24,128]{1,0:T(8,128)S(1)} %copy-done.2, bf16[3072,1280]{1,0:T(8,128)(2,1)} %bitcast.2, bf16[3072,512]{1,0:T(8,128)(2,1)} %bitcast.3, f32[1280,512]{1,0:T(8,128)S(1)} %copy-done.1, f32[1280,512]{1,0:T(8,128)S(1)} %copy-done, f32[1280,512]{1,0:T(8,128)} %m_ref.1, ...), custom_call_target="tpu_custom_call" | custom-call | flops 4026531840 | bytes 31981568 | tf_op jit(solution)/shard_map/update/pallas_call | solution.py:393
  217.4 0.0 copy-done.3
  217.4 1.5 copy.15
Async XLA Ops:
  0.6 199.7 %copy-start = (f32[1280,512]{1,0:T(8,128)S(1)}, f32[1280,512]{1,0:T(8,128)}, u32[]{:S(2)}) copy-start(f32[1280,512]{1,0:T(8,128)} %n_ref.1) | copy-start | bytes 7864324
  200.4 1.7 copy-start.1
  202.1 0.7 copy-start.2
  202.8 14.6 %copy-start.3 = (f32[1280,512]{1,0:T(8,128)S(1)}, f32[1280,512]{1,0:T(8,128)}, u32[]{:S(2)}) copy-start(f32[1280,512]{1,0:T(8,128)} %get-tuple-element.27) | copy-start | bytes 7864324

commit v4 on v3

--- a/solution.py
+++ b/solution.py
@@ -21,6 +21,18 @@
 
 MESH = pl.DeviceIdType.MESH
 CORES = 2
+
+
+def pieces_of(public_rows, private_rows):
+    cut = 3 if private_rows % 48 == 0 else 1
+    private = private_rows // cut
+    return [(0, 0, public_rows)] + [(1, at * private, private) for at in range(cut)]
+
+
+def dense(parts):
+    if parts[0].shape[0] % 16 == 0:
+        return jnp.concatenate(parts, axis=0)
+    return jnp.concatenate([part.astype(jnp.float32) for part in parts], axis=0).astype(parts[0].dtype)
 
 
 def errors_kernel(
@@ -46,6 +58,15 @@
         (prv_x, prv_t, prv_all, prv_d, prv_aims, prv_send, prv_recv, prv_own, prv_y),
     )
 
+    pieces = pieces_of(pub_all.shape[2], prv_all.shape[2])
+    last = len(pieces) - 1
+
+    def run(f):
+        return pl.ds(pieces[f][1], pieces[f][2])
+
+    def side(f):
+        return phases[pieces[f][0]]
+
     def to(src, dst, sent, got, replica, tile):
         return pltpu.make_async_remote_copy(
             src_ref=src, dst_ref=dst, send_sem=sent, recv_sem=got,
@@ -60,7 +81,7 @@
         return jnp.where(i <= 2 * inner, paired, rest)
 
     def token_copy(f, q, sent, replica):
-        ref = phases[f][2].at[q]
+        ref = side(f)[2].at[q, :, run(f)]
         return to(ref, ref, sent, x_recv.at[f, q], replica, t)
 
     def aim_copy(f, d):
@@ -71,17 +92,17 @@
     def part_copy(f, q, d):
         there = (t + d) % tiles
         return to(
-            phases[f][5].at[q, there], phases[f][6].at[q, d - 1],
+            side(f)[5].at[q, there, run(f)], side(f)[6].at[q, d - 1, run(f)],
             rs_sent.at[f, q, d - 1], rs_recv.at[f, q, d - 1], r, there,
         )
 
     def error_copy(f, q, d):
         there = (t + d) % tiles
-        ref = phases[f][3].at[q, t]
+        ref = side(f)[3].at[q, t, run(f)]
         return to(ref, ref, ag_sent.at[f, q, d - 1], ag_recv.at[f, q, d - 1], r, there)
 
     def error_arrival(f, q, d):
-        ref = phases[f][3].at[q, (t + tiles - d) % tiles]
+        ref = side(f)[3].at[q, (t + tiles - d) % tiles, run(f)]
         return to(ref, ref, ag_sent.at[f, q, d - 1], ag_recv.at[f, q, d - 1], r, (t + tiles - d) % tiles)
 
     barrier = pltpu.get_barrier_semaphore()
@@ -91,12 +112,16 @@
         pl.semaphore_signal(barrier, inc=1, device_id=(r, (t + d) % tiles), device_id_type=MESH)
     pub_all[r] = pub_x[...]
     examples = counts.shape[1]
-    seq_len = prv_x.shape[0] // examples
-    row = lax.broadcasted_iota(jnp.int32, (seq_len, 1), 0)
-    for e in range(examples):
-        live = (row < counts[0, e]).astype(jnp.float32)
-        at = slice(e * seq_len, (e + 1) * seq_len)
-        prv_all[r, at, :] = (prv_x[at, :].astype(jnp.float32) * live).astype(jnp.bfloat16)
+    sub = prv_x.shape[1]
+    seq_len = tiles * sub // examples
+    for at in range(tiles):
+        slot = at * sub + lax.broadcasted_iota(jnp.int32, (sub, 1), 0)
+        live = jnp.zeros((sub, 1), jnp.float32)
+        for e in range(examples):
+            first = e * seq_len
+            inside = jnp.logical_and(slot >= first, slot < first + counts[0, e])
+            live = jnp.where(inside, 1.0, live)
+        prv_all[r, at] = (prv_x[at].astype(jnp.float32) * live).astype(jnp.bfloat16)
     w_ref[...] = weight[...].astype(jnp.bfloat16)
     pl.semaphore_wait(barrier, replicas + tiles - 2)
 
@@ -124,38 +149,47 @@
             token_copy(f, mine, down_sem.at[f, i], r - CORES).wait_send()
 
     def partial(f, q):
-        x_all, send, own, y = phases[f][2], phases[f][5], phases[f][7], phases[f][8]
-        sub = y.shape[1]
-        out = jnp.dot(x_all[q], w_ref[...], preferred_element_type=jnp.float32)
+        _, _, x_all, _, _, send, _, own, y = side(f)
+        _, first, count = pieces[f]
+        stop = first + count
+        tokens = dense([x_all[q, at, first:stop] for at in range(tiles)])
+        out = jnp.dot(tokens, w_ref[...], preferred_element_type=jnp.float32)
         for at in range(tiles):
-            part = out[at * sub : (at + 1) * sub]
-            y[at] = part
-            send[q, at] = part.astype(jnp.bfloat16)
+            part = out[at * count : (at + 1) * count]
+            y[at, first:stop] = part
+            send[q, at, first:stop] = part.astype(jnp.bfloat16)
         for d in range(1, tiles):
             part_copy(f, q, d).start()
-        own[q] = y[t]
+        own[q, first:stop] = y[t, first:stop]
 
     def finish(f, q):
-        d_all, aims, recv, own = phases[f][3], phases[f][4], phases[f][6], phases[f][7]
+        _, targets, _, d_all, aims, _, recv, own, _ = side(f)
+        a, first, count = pieces[f]
+        stop = first + count
         gap = (r + replicas - q) % replicas
 
         @pl.when(gap > 0)
         def _():
-            to(aims.at[gap - 1], aims.at[gap - 1], aim_sent.at[f, gap - 1], aim_recv.at[f, gap - 1], q, t).wait_recv()
-            own[q] = own[q] - aims[gap - 1].astype(jnp.float32)
+            if first == 0:
+                to(aims.at[gap - 1], aims.at[gap - 1], aim_sent.at[a, gap - 1], aim_recv.at[a, gap - 1], q, t).wait_recv()
+            own[q, first:stop] = own[q, first:stop] - aims[gap - 1, first:stop].astype(jnp.float32)
 
         @pl.when(gap == 0)
         def _():
-            mine = phases[f][1][:, pl.ds(pl.multiple_of(r * cols, cols), cols)]
-            own[q] = own[q] - mine.astype(jnp.float32)
-
-        total = own[q]
+            mine = targets[first:stop, pl.ds(pl.multiple_of(r * cols, cols), cols)]
+            own[q, first:stop] = own[q, first:stop] - mine.astype(jnp.float32)
+
+        total = own[q, first:stop]
         for d in range(1, tiles):
             part_copy(f, q, d).wait_recv()
-            total = total + recv[q, d - 1].astype(jnp.float32)
-        d_all[q, t] = total.astype(jnp.bfloat16)
+            total = total + recv[q, d - 1, first:stop].astype(jnp.float32)
+        d_all[q, t, first:stop] = total.astype(jnp.bfloat16)
         for d in range(1, tiles):
             error_copy(f, q, d).start()
+
+    def finish_chip(f, chip):
+        finish(f, chip * CORES + c)
+        finish(f, chip * CORES + 1 - c)
 
     def arrived(f, q):
         for d in range(1, tiles):
@@ -170,10 +204,10 @@
             return carry
 
         lax.fori_loop(0, replicas, waiting, 0)
-        total = replicas * pub_x.shape[0]
+        total = replicas * tiles * pub_x.shape[1]
         errors = pub_d[...].reshape(total, cols)
         for at in range(0, rows, step):
-            tokens = pub_all[:, :, at : at + step].reshape(total, step)
+            tokens = pub_all[:, :, :, at : at + step].reshape(total, step)
             grads = lax.dot_general(tokens, errors, contract_rows, preferred_element_type=jnp.float32)
             grads = grads * (1.0 / root)
             moved = beta_public * moment[at : at + step, :] + (1.0 - beta_public) * grads * grads
@@ -183,24 +217,21 @@
     def norms(chip):
         def body(which, carry):
             q = chip * CORES + (c + which) % CORES
-            arrived(1, q)
-            parts = [prv_d[q, at] for at in range(tiles)]
-            if parts[0].shape[0] % 16 == 0:
-                errors = jnp.concatenate(parts, axis=0)
-            else:
-                errors = jnp.concatenate([part.astype(jnp.float32) for part in parts], axis=0)
-                errors = errors.astype(jnp.bfloat16)
-            for e in range(examples):
-                span = slice(e * seq_len, (e + 1) * seq_len)
-                total = jnp.zeros((8, cols), jnp.float32)
-                for at in range(0, rows, step):
+            for f in range(1, last + 1):
+                arrived(f, q)
+            errors = dense([prv_d[q, at] for at in range(tiles)])
+            totals = [jnp.zeros((8, cols), jnp.float32)] * examples
+            for at in range(0, rows, step):
+                tokens = dense([prv_all[q, own_rows, :, at : at + step] for own_rows in range(tiles)])
+                for e in range(examples):
+                    span = slice(e * seq_len, (e + 1) * seq_len)
                     grads = lax.dot_general(
-                        prv_all[q, span, at : at + step], errors[span],
-                        contract_rows, preferred_element_type=jnp.float32,
+                        tokens[span], errors[span], contract_rows, preferred_element_type=jnp.float32
                     )
                     scaled = grads * precond[at : at + step, :]
-                    total += jnp.sum((scaled * scaled).reshape(step // 8, 8, cols), axis=0)
-                line = jnp.sum(total, axis=0, keepdims=True)
+                    totals[e] = totals[e] + jnp.sum((scaled * scaled).reshape(step // 8, 8, cols), axis=0)
+            for e in range(examples):
+                line = jnp.sum(totals[e], axis=0, keepdims=True)
                 line = sum(line[:, at : at + 128] for at in range(0, cols, 128))
                 squares[pl.ds(q * examples + e, 1), :] = line
             return carry
@@ -235,41 +266,46 @@
                         along(f, i, chip)
                 token_copy(f, mine, core_sem.at[f, i], z * CORES + 1 - c).start()
 
-                @pl.when(i == 0)
-                def _():
-                    for d in range(1, replicas):
-                        aim_copy(f, d).start()
-
-                if f == 0:
+                if pieces[f][1] == 0:
+                    @pl.when(i == 0)
+                    def _():
+                        for d in range(1, replicas):
+                            aim_copy(pieces[f][0], d).start()
+
+                if f < last:
                     @pl.when(i == min(1, chips - 1))
                     def _():
-                        along(1, 0, z)
+                        along(f + 1, 0, z)
 
                 partial(f, mine)
                 token_copy(f, other, core_sem.at[f, i], r).wait_recv()
                 partial(f, other)
 
+            if f > 0:
+                @pl.when(i == 0)
+                def _():
+                    finish_chip(f - 1, chip_at(chips - 1))
+
             @pl.when(jnp.logical_and(i > 0, i <= chips))
             def _():
-                chip = chip_at(i - 1)
-                finish(f, chip * CORES + c)
-                finish(f, chip * CORES + 1 - c)
+                finish_chip(f, chip_at(i - 1))
 
             if f == 1:
                 @pl.when(i == 1)
                 def _():
                     public_update()
 
+            if f == last:
                 @pl.when(i > 1)
                 def _():
                     norms(chip_at(i - 2))
 
             return carry
 
-        lax.fori_loop(0, chips + 1 + f, body, 0)
-
-    phase(0)
-    phase(1)
+        lax.fori_loop(0, chips + 2 if f == last else chips, body, 0)
+
+    for f in range(last + 1):
+        phase(f)
 
     for d in range(1, tiles):
         tile_copy(d).start()
@@ -306,11 +342,12 @@
             return carry
 
         lax.fori_loop(0, chips, sent, 0)
-        for d in range(1, replicas):
-            aim_copy(f, d).wait_send()
-
-    close(0)
-    close(1)
+        if pieces[f][1] == 0:
+            for d in range(1, replicas):
+                aim_copy(pieces[f][0], d).wait_send()
+
+    for f in range(last + 1):
+        close(f)
 
 
 def gathered_errors(pub_x, prv_x, pub_t, prv_t, counts, weight, moment, root, clip_norm):
@@ -323,7 +360,8 @@
     subs = [span // tiles for span in spans]
     examples = counts.shape[1] * replicas
     vmem = pl.BlockSpec(memory_space=pltpu.VMEM)
-    tokens = [(replicas, span, rows) for span in spans]
+    tokens = [(replicas, tiles, sub, rows) for sub in subs]
+    count = len(pieces_of(*subs))
     errors = [(replicas, tiles, sub, cols) for sub in subs]
     scratch = [pltpu.VMEM(tokens[0], half), pltpu.VMEM(errors[0], half), pltpu.VMEM((rows, cols), half)]
     scratch += [pltpu.VMEM(shape + (examples, 128), full) for shape in ((), (tiles - 1,), (replicas - 1,))]
@@ -332,8 +370,8 @@
     scratch += [pltpu.VMEM((replicas, tiles - 1, sub, cols), half) for sub in subs]
     scratch += [pltpu.VMEM((replicas, sub, cols), full) for sub in subs]
     scratch += [pltpu.VMEM((tiles, sub, cols), full) for sub in subs]
-    sems = [(2, replicas), (2, chips), (2, chips), (2, chips), (2, replicas - 1), (2, replicas - 1)]
-    sems += [(2, replicas, tiles - 1)] * 4
+    sems = [(count, replicas)] + [(count, chips)] * 3 + [(2, replicas - 1)] * 2
+    sems += [(count, replicas, tiles - 1)] * 4
     sems += [(tiles - 1,)] * 2 + [(replicas - 1,)] * 2
     scratch += [pltpu.SemaphoreType.DMA(shape) for shape in sems]
     flops = 4 * replicas * sum(spans) * rows * cols
@@ -355,7 +393,10 @@
         ),
         cost_estimate=pl.CostEstimate(flops=flops, bytes_accessed=2 * replicas * sum(spans) * rows, transcendentals=0),
         name="gathered_errors",
-    )(pub_x, prv_x, pub_t, prv_t, counts, weight, moment)
+    )(
+        pub_x.reshape(tiles, subs[0], rows), prv_x.reshape(tiles, subs[1], rows),
+        pub_t, prv_t, counts, weight, moment,
+    )
 
 
 def update_kernel(

time: 219 us -> 204 us (0.932)
  Pallas kernels: 214 us -> 199 us
    pallas_call x1, Pallas kernels: 200 us -> 185 us  [gathered_errors(): pl.pallas_call(functools.partial(errors_kernel, root, clip_norm), out_sha...]
where the time goes in v4:
time: 204 us
  Pallas kernels  199 us (98%)
  local copies, waits for them, and re-layouts  3.94 us (2%)
    pallas_call x1, Pallas kernels, gathered_errors(): pl.pallas_call(functools.partial(errors_kernel, root, clip_norm), out_sha...  185 us
    pallas_call x1, Pallas kernels, update(): pl.pallas_call(functools.partial(update_kernel, examples, noise_scale), g...  14.6 us

profile of v4, /device:TPU:0, one launch (start us, length us, event | category | flops | bytes accessed | tf_op | source)
XLA Modules:
  0.0 203.8 jit_solution(10782689122019888599)
XLA Ops:
  0.6 0.0 copy-start
  0.6 184.6 %gathered_errors.1 = (bf16[8,4,96,1280]{3,2,1,0:T(8,128)(2,1)}, bf16[8,4,96,512]{3,2,1,0:T(8,128)(2,1)}, f32[1280,512]{1,0:T(8,128)}, f32[1280,512]{1,0:T(8,128)}, f32[24,128]{1,0:T(8,128)}) custom-call(bf16[4,64,1280]{2,1,0:T(8,128)(2,1)} %bitcast.7, bf16[4,96,1280]{2,1,0:T(8,128)(2,1)} %bitcast.6, bf16[64,4096]{1,0:T(8,128)(2,1)} %pub_t.1, ...), custom_call_target="tpu_custom_call" | custom-call | flops 13421772800 | bytes 13107200 | tf_op jit(solution)/shard_map/gathered_errors/pallas_call | solution.py:379
  185.2 0.0 copy-done
  185.2 0.0 copy-start.1
  185.2 1.7 copy-done.1
  187.0 0.0 copy-start.2
  187.0 0.7 copy-done.2
  187.7 0.0 copy-start.3
  187.7 14.6 %update.1 = (f32[1280,512]{1,0:T(8,128)}, f32[1280,512]{1,0:T(8,128)}, f32[1280,512]{1,0:T(8,128)}) custom-call(f32[24,128]{1,0:T(8,128)S(1)} %copy-done.2, bf16[3072,1280]{1,0:T(8,128)(2,1)} %bitcast.4, bf16[3072,512]{1,0:T(8,128)(2,1)} %bitcast.5, f32[1280,512]{1,0:T(8,128)S(1)} %copy-done.1, f32[1280,512]{1,0:T(8,128)S(1)} %copy-done, f32[1280,512]{1,0:T(8,128)} %m_ref.1, ...), custom_call_target="tpu_custom_call" | custom-call | flops 4026531840 | bytes 31981568 | tf_op jit(solution)/shard_map/update/pallas_call | solution.py:434
  202.3 0.0 copy-done.3
  202.3 1.5 copy.15
Async XLA Ops:
  0.6 184.6 %copy-start = (f32[1280,512]{1,0:T(8,128)S(1)}, f32[1280,512]{1,0:T(8,128)}, u32[]{:S(2)}) copy-start(f32[1280,512]{1,0:T(8,128)} %n_ref.1) | copy-start | bytes 7864324
  185.2 1.7 copy-start.1
  187.0 0.7 copy-start.2
  187.7 14.6 %copy-start.3 = (f32[1280,512]{1,0:T(8,128)S(1)}, f32[1280,512]{1,0:T(8,128)}, u32[]{:S(2)}) copy-start(f32[1280,512]{1,0:T(8,128)} %get-tuple-element.27) | copy-start | bytes 7864324

commit v5 on v4

--- a/solution.py
+++ b/solution.py
@@ -38,8 +38,8 @@
 def errors_kernel(
     root, clip_norm,
     pub_x, prv_x, pub_t, prv_t, counts, weight, moment,
-    prv_all, prv_d, new_public, precond, factors,
-    pub_all, pub_d, w_ref, squares, tile_squares, all_squares,
+    prv_all, prv_d, new_public, factors,
+    pub_all, pub_d, w_ref, precond, squares, tile_squares, all_squares,
     pub_aims, prv_aims, pub_send, prv_send, pub_recv, prv_recv, pub_own, prv_own, pub_y, prv_y,
     x_recv, up_sem, down_sem, core_sem, aim_recv, aim_sent, rs_recv, rs_sent, ag_recv, ag_sent,
     tile_recv, tile_sent, all_recv, all_sent,
@@ -272,10 +272,12 @@
                         for d in range(1, replicas):
                             aim_copy(pieces[f][0], d).start()
 
-                if f < last:
+                ahead = [g for g in ((1, 2) if f == 0 else (f + 2,)) if g <= last]
+                if ahead:
                     @pl.when(i == min(1, chips - 1))
                     def _():
-                        along(f + 1, 0, z)
+                        for g in ahead:
+                            along(g, 0, z)
 
                 partial(f, mine)
                 token_copy(f, other, core_sem.at[f, i], r).wait_recv()
@@ -364,6 +366,7 @@
     count = len(pieces_of(*subs))
     errors = [(replicas, tiles, sub, cols) for sub in subs]
     scratch = [pltpu.VMEM(tokens[0], half), pltpu.VMEM(errors[0], half), pltpu.VMEM((rows, cols), half)]
+    scratch += [pltpu.VMEM((rows, cols), full)]
     scratch += [pltpu.VMEM(shape + (examples, 128), full) for shape in ((), (tiles - 1,), (replicas - 1,))]
     scratch += [pltpu.VMEM((replicas - 1, sub, cols), half) for sub in subs]
     scratch += [pltpu.VMEM((replicas, tiles, sub, cols), half) for sub in subs]
@@ -382,11 +385,10 @@
             jax.ShapeDtypeStruct(tokens[1], half),
             jax.ShapeDtypeStruct(errors[1], half),
             state,
-            state,
             jax.ShapeDtypeStruct((examples, 128), full),
         ],
         in_specs=[vmem] * 4 + [pl.BlockSpec(memory_space=pltpu.SMEM)] + [vmem] * 2,
-        out_specs=[vmem] * 5,
+        out_specs=[vmem] * 4,
         scratch_shapes=scratch,
         compiler_params=pltpu.CompilerParams(
             collective_id=0, has_side_effects=True, vmem_limit_bytes=58 * 1024 * 1024
@@ -401,7 +403,7 @@
 
 def update_kernel(
     total_examples, noise_scale, f_ref, x_ref, d_ref, p_ref, n_ref, m_ref, v_ref, w_ref,
-    new_w, new_m, new_v, weighted,
+    new_w, new_m, new_v, new_p, weighted,
 ):
     examples = f_ref.shape[0]
     seq_len = d_ref.shape[0] // examples
@@ -412,7 +414,9 @@
             at = slice(j * seq_len, (j + 1) * seq_len)
             weighted[at, :] = (f_ref[j : j + 1, :1] * d_ref[at, :].astype(jnp.float32)).astype(jnp.bfloat16)
 
-    summed = p_ref[...] * lax.dot_general(
+    new_p[...] = p_ref[...]
+    precond = 1.0 / (jnp.sqrt(p_ref[...]) + public_epsilon)
+    summed = precond * lax.dot_general(
         x_ref[...], weighted[...], contract_rows, preferred_element_type=jnp.float32
     )
     gradient = (summed + noise_scale * n_ref[...]) * (1.0 / total_examples)
@@ -425,7 +429,7 @@
     new_w[...] = w_ref[...] - learn_rate * first_hat / (jnp.sqrt(second_hat) + adam_epsilon)
 
 
-def update(factors, tokens, delta, precond, noise, first, second, weight, noise_scale):
+def update(factors, tokens, delta, public, noise, first, second, weight, noise_scale):
     slots, rows = tokens.shape
     cols = delta.shape[1]
     examples = factors.shape[0]
@@ -440,8 +444,8 @@
             pl.BlockSpec((slots, cols), lambda i: (0, 0)),
         ]
         + [state] * 5,
-        out_specs=[state] * 3,
-        out_shape=[jax.ShapeDtypeStruct((rows, cols), jnp.float32)] * 3,
+        out_specs=[state] * 4,
+        out_shape=[jax.ShapeDtypeStruct((rows, cols), jnp.float32)] * 4,
         scratch_shapes=[pltpu.VMEM((slots, cols), jnp.bfloat16)],
         compiler_params=pltpu.CompilerParams(vmem_limit_bytes=48 * 1024 * 1024),
         cost_estimate=pl.CostEstimate(
@@ -450,7 +454,7 @@
             transcendentals=rows * cols,
         ),
         name="update",
-    )(factors, tokens, delta, precond, noise, first, second, weight)
+    )(factors, tokens, delta, public, noise, first, second, weight)
 
 
 def on_device(
@@ -476,15 +480,15 @@
     public_total = public_tokens.shape[0] * replicas
 
     clip_norm = clip_factor * math.sqrt(seq_len * width * columns)
-    private_all, private_delta, new_public, precond, factors = gathered_errors(
+    private_all, private_delta, new_public, factors = gathered_errors(
         public_tokens, private_tokens, public_targets, private_targets, token_counts, weight, public_moment,
         math.sqrt(public_total), clip_norm,
     )
     private_all = private_all.reshape(slots_here * replicas, -1)
     private_delta = private_delta.reshape(slots_here * replicas, cols)
     noise_scale = noise_level * clip_factor * math.sqrt(seq_len)
-    new_weight, new_first, new_second = update(
-        factors, private_all, private_delta, precond, noise_draw, adam_first, adam_second, weight, noise_scale
+    new_weight, new_first, new_second, new_public = update(
+        factors, private_all, private_delta, new_public, noise_draw, adam_first, adam_second, weight, noise_scale
     )
     return (new_weight, new_first, new_second, new_public)
 

time: 204 us -> 210 us (1.029)
  Pallas kernels: 199 us -> 206 us
    pallas_call x1, Pallas kernels: 185 us -> 191 us  [gathered_errors(): pl.pallas_call(functools.partial(errors_kernel, root, clip_norm), out_sha...]
where the time goes in v5:
time: 210 us
  Pallas kernels  206 us (98%)
  local copies, waits for them, and re-layouts  2.44 us (1%)
    pallas_call x1, Pallas kernels, gathered_errors(): pl.pallas_call(functools.partial(errors_kernel, root, clip_norm), out_sha...  191 us
    pallas_call x1, Pallas kernels, update(): pl.pallas_call(functools.partial(update_kernel, examples, noise_scale), g...  15.7 us

profile of v5, /device:TPU:0, one launch (start us, length us, event | category | flops | bytes accessed | tf_op | source)
XLA Modules:
  0.0 209.6 jit_solution(5753039639059042246)
XLA Ops:
  0.6 0.0 copy-start
  0.6 190.8 %gathered_errors.1 = (bf16[8,4,96,1280]{3,2,1,0:T(8,128)(2,1)}, bf16[8,4,96,512]{3,2,1,0:T(8,128)(2,1)}, f32[1280,512]{1,0:T(8,128)}, f32[24,128]{1,0:T(8,128)}) custom-call(bf16[4,64,1280]{2,1,0:T(8,128)(2,1)} %bitcast.7, bf16[4,96,1280]{2,1,0:T(8,128)(2,1)} %bitcast.6, bf16[64,4096]{1,0:T(8,128)(2,1)} %pub_t.1, bf16[96,4096]{1,0:T(8,128)(2,1)} %prv_t.1, ...), custom_call_target="tpu_custom_call" | custom-call | flops 13421772800 | bytes 13107200 | tf_op jit(solution)/shard_map/gathered_errors/pallas_call | solution.py:382
  191.5 0.0 copy-done
  191.5 0.0 copy-start.1
  191.5 1.7 copy-done.1
  193.2 0.0 copy-start.2
  193.2 0.7 copy-done.2
  193.9 15.7 %update.1 = (f32[1280,512]{1,0:T(8,128)}, f32[1280,512]{1,0:T(8,128)}, f32[1280,512]{1,0:T(8,128)}, f32[1280,512]{1,0:T(8,128)}) custom-call(f32[24,128]{1,0:T(8,128)S(1)} %copy-done.2, bf16[3072,1280]{1,0:T(8,128)(2,1)} %bitcast.4, bf16[3072,512]{1,0:T(8,128)(2,1)} %bitcast.5, f32[1280,512]{1,0:T(8,128)S(1)} %copy-done.1, f32[1280,512]{1,0:T(8,128)S(1)} %copy-done, ...), custom_call_target="tpu_custom_call" | custom-call | flops 4026531840 | bytes 31981568 | tf_op jit(solution)/shard_map/update/pallas_call | solution.py:438
Async XLA Ops:
  0.6 190.8 %copy-start = (f32[1280,512]{1,0:T(8,128)S(1)}, f32[1280,512]{1,0:T(8,128)}, u32[]{:S(2)}) copy-start(f32[1280,512]{1,0:T(8,128)} %n_ref.1) | copy-start | bytes 7864324
  191.5 1.7 copy-start.1
  193.2 0.7 copy-start.2
